TPU v7x, 512 devices: a whole 4x8x8 slice. The times are simulated.
512 devices in a mesh: seq: 128 (over x, y_lo, z, core), head: 4 (over y_hi).
Axes of the slice: x: 4, y: 8 (y_hi: 4, y_lo: 2; y = y_hi * 2 + y_lo), z: 8, core: 2. Of those that a mesh axis runs over, the one named last changes fastest.
Arguments:
- tokens: bfloat16 [32768, 768], P('seq'), may hold values from -9 to 9
- valid: int32 [32768], P('seq'), may hold values from 0 to 1, as said below
- offsets: int32 [16, 2], P('head'), may hold values from 0 to 15, as said below
- qkv_weight: bfloat16 [768, 2304], P(None, 'head'), may hold values from -0.21875 to 0.21875
- out_weight: bfloat16 [768, 768], P('head'), may hold values from -0.21875 to 0.21875
- out_grad: bfloat16 [32768, 768], P('seq'), may hold values from -6 to 6
Outputs:
- grad_tokens: bfloat16 [32768, 768], P('seq', 'head')
- grad_qkv_weight: float32 [768, 2304], P('seq', 'head')
- grad_out_weight: float32 [768, 768], P('head', 'seq')
Inputs may be any that keep to these rules, and one draw needn't show every extreme that they name: `valid`: for every j, among the tokens 256 * j to 256 * (j + 1) - 1 at least one is 1. `offsets`: column 0 lies in 0 to 3, column 1 in 0 to 15.
All inputs are finite; a program needn't handle non-finite values.
Results may differ from a plain program's by a relative error of at most 0.03.
The roundings to bfloat16 on the way count: a program that leaves them out, or rounds other values in their place, can miss the bound.
Values may be sent and summed in bfloat16 or wider, within the bound.
A program may use at most 64 MiB of HBM per device.

v0:
```python
import math

import jax
import jax.numpy as jnp
from jax import lax
from jax.sharding import PartitionSpec as P

SPAN2 = 4


def swapped(block, axis, apart):
    count = lax.axis_size(axis)
    route = []
    for low in range(count):
        high = low | 1 << apart
        if high != low and high < count:
            route += [(low, high), (high, low)]
    return lax.ppermute(block, axis, route)


def chosen_mask(stride, phases, extra_dims):
    chosen = jnp.arange(stride, dtype=jnp.int32)[:, None] == phases[None, :]
    return chosen.reshape((1, stride, phases.shape[0]) + (1,) * extra_dims)


def select_rows(values, stride, phases):
    if stride == 1:
        return values
    blocks = values.reshape((values.shape[0] // stride, stride) + values.shape[1:])
    chosen = chosen_mask(stride, phases, values.ndim - 2)
    return jnp.sum(jnp.where(chosen, blocks, jnp.zeros((), values.dtype)), axis=1)


def spread_rows(values, stride, phases, filler):
    if stride == 1:
        return values
    chosen = chosen_mask(stride, phases, values.ndim - 2)
    full = jnp.where(chosen, values[:, None], filler)
    return full.reshape((values.shape[0] * stride,) + values.shape[1:])


def per_device(tokens, valid, offsets, qkv_weight, out_weight, out_grad):
    rows_here = tokens.shape[0]
    heads_here = offsets.shape[0]
    head_size = qkv_weight.shape[1] // (3 * heads_here)
    factor = 1.0 / math.sqrt(head_size)
    span_far = min(16, lax.axis_size("seq"))
    far_steps = span_far.bit_length() - 1
    near_steps = SPAN2.bit_length() - 1
    projected = jnp.dot(tokens, qkv_weight, preferred_element_type=jnp.float32).astype(jnp.bfloat16)
    projected = projected.reshape(rows_here, heads_here, 3, head_size)
    queries = projected[:, :, 0]
    key_value = projected[:, :, 1:]
    live_keys = jnp.broadcast_to((valid > 0)[:, None], (rows_here, heads_here)).astype(jnp.bfloat16)
    near_phase = offsets[:, 0]
    far_phase = offsets[:, 1]
    near_query = select_rows(queries, SPAN2, near_phase)
    far_query = select_rows(queries, span_far, far_phase)
    near_pairs = select_rows(key_value, SPAN2, near_phase)
    near_live = select_rows(live_keys, SPAN2, near_phase)
    far_pairs = select_rows(key_value, span_far, far_phase)
    far_live = select_rows(live_keys, span_far, far_phase)
    bit_order = list(range(far_steps))
    record = []
    for which_bit in bit_order:
        with_near = which_bit < near_steps
        near_len = near_pairs.shape[0]
        far_len = far_pairs.shape[0]
        record.append((which_bit, with_near, near_len, far_len))
        if with_near:
            send_pairs = jnp.concatenate([near_pairs, far_pairs], axis=0)
            send_live = jnp.concatenate([near_live, far_live], axis=0)
        else:
            send_pairs = far_pairs
            send_live = far_live
        recv_pairs, recv_live = swapped((send_pairs, send_live), "seq", which_bit)
        if with_near:
            near_pairs = jnp.concatenate([near_pairs, recv_pairs[:near_len]], axis=0)
            near_live = jnp.concatenate([near_live, recv_live[:near_len]], axis=0)
            far_pairs = jnp.concatenate([far_pairs, recv_pairs[near_len:]], axis=0)
            far_live = jnp.concatenate([far_live, recv_live[near_len:]], axis=0)
        else:
            far_pairs = jnp.concatenate([far_pairs, recv_pairs], axis=0)
            far_live = jnp.concatenate([far_live, recv_live], axis=0)
    level_data = [
        (queries, key_value, live_keys, 1, near_phase),
        (near_query, near_pairs, near_live, SPAN2, near_phase),
        (far_query, far_pairs, far_live, span_far, far_phase),
    ]
    score_list = []
    mask_list = []
    top_score = None
    for dilation_level_query, dilation_level_pairs, level_live, stride, phases in level_data:
        scores = (
            jnp.einsum(
                "xsr,vsr->xsv",
                dilation_level_query,
                dilation_level_pairs[:, :, 0],
                preferred_element_type=jnp.float32,
            )
            * factor
        )
        key_mask = (level_live.T > 0)[None]
        row_max = jnp.max(jnp.where(key_mask, scores, -1e30), axis=-1)
        score_list.append(scores)
        mask_list.append(key_mask)
        if top_score is None:
            top_score = row_max
        else:
            top_score = jnp.maximum(top_score, spread_rows(row_max, stride, phases, -1e30))
    numer = jnp.zeros((rows_here, heads_here, head_size), jnp.float32)
    denom = jnp.zeros((rows_here, heads_here), jnp.float32)
    weight_list = []
    for level_idx in range(3):
        dilation_level_query, dilation_level_pairs, level_live, stride, phases = level_data[
            level_idx
        ]
        top_at = select_rows(top_score, stride, phases)
        weights = jnp.where(
            mask_list[level_idx], jnp.exp(score_list[level_idx] - top_at[..., None]), 0.0
        )
        weight_list.append(weights)
        numer_part = jnp.einsum(
            "obv,vby->oby",
            weights.astype(jnp.bfloat16),
            dilation_level_pairs[:, :, 1],
            preferred_element_type=jnp.float32,
        )
        numer = numer + spread_rows(numer_part, stride, phases, 0.0)
        denom = denom + spread_rows(jnp.sum(weights, axis=-1), stride, phases, 0.0)
    attention = (numer / denom[..., None]).astype(jnp.bfloat16)
    attention_flat = attention.reshape(rows_here, heads_here * head_size)
    d_attention = jnp.dot(out_grad, out_weight.T, preferred_element_type=jnp.float32).astype(
        jnp.bfloat16
    )
    d_attention = d_attention.reshape(rows_here, heads_here, head_size)
    delta = jnp.sum(d_attention.astype(jnp.float32) * attention.astype(jnp.float32), axis=-1)
    query_gradient_rows = jnp.zeros((rows_here, heads_here, head_size), jnp.float32)
    own_grad = None
    remote_grads = []
    for level_idx in range(3):
        dilation_level_query, dilation_level_pairs, level_live, stride, phases = level_data[
            level_idx
        ]
        den_at = select_rows(denom, stride, phases)
        normalized_scores = weight_list[level_idx] / den_at[..., None]
        selected_delta_grad = select_rows(d_attention, stride, phases)
        delta_sel = select_rows(delta, stride, phases)
        prob_grad = jnp.einsum(
            "xsr,vsr->xsv",
            selected_delta_grad,
            dilation_level_pairs[:, :, 1],
            preferred_element_type=jnp.float32,
        )
        score_gradient = (normalized_scores * (prob_grad - delta_sel[..., None])).astype(
            jnp.bfloat16
        )
        q_part = (
            jnp.einsum(
                "obv,vby->oby",
                score_gradient,
                dilation_level_pairs[:, :, 0],
                preferred_element_type=jnp.float32,
            )
            * factor
        )
        k_part = (
            jnp.einsum(
                "tqs,tqg->sqg",
                score_gradient,
                dilation_level_query,
                preferred_element_type=jnp.float32,
            )
            * factor
        )
        v_part = jnp.einsum(
            "tqs,tqg->sqg",
            normalized_scores.astype(jnp.bfloat16),
            selected_delta_grad,
            preferred_element_type=jnp.float32,
        )
        query_gradient_rows = query_gradient_rows + spread_rows(q_part, stride, phases, 0.0)
        pair_grad = jnp.stack([k_part, v_part], axis=2)
        if level_idx == 0:
            own_grad = pair_grad
        else:
            remote_grads.append(pair_grad)
    near_grad, far_grad = remote_grads
    for which_bit, with_near, near_len, far_len in reversed(record):
        if with_near:
            send_back = jnp.concatenate([near_grad[near_len:], far_grad[far_len:]], axis=0)
        else:
            send_back = far_grad[far_len:]
        returned = swapped(send_back.astype(jnp.bfloat16), "seq", which_bit).astype(send_back.dtype)
        if with_near:
            near_grad = near_grad[:near_len] + returned[:near_len]
            far_grad = far_grad[:far_len] + returned[near_len:]
        else:
            far_grad = far_grad[:far_len] + returned
    own_grad = (
        own_grad
        + spread_rows(near_grad, SPAN2, near_phase, 0.0)
        + spread_rows(far_grad, span_far, far_phase, 0.0)
    )
    qkv_grads = jnp.concatenate([query_gradient_rows[:, :, None], own_grad], axis=2).astype(
        jnp.bfloat16
    )
    qkv_grads = qkv_grads.reshape(rows_here, 3 * heads_here * head_size)
    partial_sum = jnp.dot(qkv_grads, qkv_weight.T, preferred_element_type=jnp.float32)
    grad_tokens = lax.psum_scatter(
        partial_sum.astype(jnp.bfloat16), "head", scatter_dimension=1, tiled=True
    )
    reduced_row_pairs = (((0,), (0,)), ((), ()))
    grad_qkv_weight = lax.psum_scatter(
        lax.dot_general(tokens, qkv_grads, reduced_row_pairs, preferred_element_type=jnp.float32),
        "seq",
        scatter_dimension=0,
        tiled=True,
    )
    out_term = lax.dot_general(
        attention_flat, out_grad, reduced_row_pairs, preferred_element_type=jnp.float32
    )
    grad_out_weight = lax.psum_scatter(out_term, "seq", scatter_dimension=1, tiled=True)
    return (grad_tokens, grad_qkv_weight, grad_out_weight)


def solution(mesh):
    return jax.shard_map(
        per_device,
        mesh=mesh,
        in_specs=(
            P("seq", None),
            P("seq"),
            P("head", None),
            P(None, "head"),
            P("head", None),
            P("seq", None),
        ),
        out_specs=(P("seq", "head"), P("seq", "head"), P("head", "seq")),
        check_vma=False,
    )
```

profile of v0, /device:TPU:1, one launch (start us, length us, event | category | flops | bytes accessed | tf_op | source)
XLA Modules:
  0.0 1225.3 jit_solution(8181901045349646396)
XLA Ops:
  10.2 8.8 collective-permute-start
  19.0 1.4 convolution_convert_fusion.1
  23.0 12.8 %collective-permute-start.2 = (bf16[80,4,2,48]{0,3,1,2:T(8,128)(2,1)}, bf16[80,4,2,48]{0,3,1,2:T(8,128)(2,1)S(1)}, u32[]{:S(2)}, u32[]{:S(2)}) collective-permute-start(bf16[80,4,2,48]{0,3,1,2:T(8,128)(2,1)} %pad_maximum_fusion.6), channel_id=1, source_target_pairs={{0,4},{4,0},{8,12},{12,8},{16,20},{20,16},{24,28},{28,24},{32,36},... | collective-permute-start | bytes 184328 | tf_op jit(solution)/shard_map/ppermute | solution.py:18
  37.7 3.8 collective-permute-start.1
  41.5 1.5 fusion.38
  43.3 5.1 collective-permute-start.4
  50.0 6.8 collective-permute-start.5
  58.6 2.7 collective-permute-start.3
  61.3 3.7 collective-permute-done.3
  65.2 3.6 collective-permute-start.6
  68.9 3.6 collective-permute-done.6
  73.3 6.9 collective-permute-start.7
  80.7 2.2 collective-permute-done.7
  82.9 1.8 concatenate.73
  84.6 1.1 select_reduce_fusion.9
  86.6 1.7 convolution_bitcast_fusion.9
  97.2 1.7 convolution_bitcast_fusion.3
  101.4 1.1 select_reduce_fusion.6
  107.4 7.0 collective-permute-start.8
  114.7 2.1 collective-permute-done.8
  116.9 5.0 collective-permute-start.9
  123.2 3.1 collective-permute-done.9
  127.3 1.9 collective-permute-start.10
  129.3 1.1 fusion.20
  130.4 4.4 collective-permute-done.10
  135.2 10.0 collective-permute-start.11
  148.4 1.6 convolution_bitcast_fusion
  150.5 1.3 convolution_convert_fusion
  151.8 309.7 %fusion = f32[192,8]{0,1:T(8,128)S(1)} fusion(f32[192,768]{0,1:T(8,128)S(1)} %fusion.74), kind=kCustom, calls=%all-reduce-scatter | all-reduce-scatter fusion | flops 196609 | bytes 598016
  461.5 1.3 collective-permute-start.42
  462.8 1.3 collective-permute-start.43
  464.1 1.3 collective-permute-start.41
  465.4 1.3 collective-permute-start.40
  466.7 1.3 collective-permute-start.39
  468.0 1.3 collective-permute-start.38
  469.3 1.3 collective-permute-start.37
  470.6 1.3 collective-permute-start.36
  471.9 1.3 collective-permute-start.35
  473.2 17.6 %collective-permute-start.34 = (f32[192,8]{0,1:T(8,128)S(1)}, f32[192,8]{0,1:T(8,128)S(1)}, u32[]{:S(2)}, u32[]{:S(2)}) collective-permute-start(f32[192,8]{0,1:T(8,128)S(1)} %fusion), channel_id=1, source_target_pairs={{0,92},{4,96},{8,100},{12,104},{16,108},{20,112},{24,116},{28,120}... | collective-permute-start | bytes 18440
  490.9 2.0 collective-permute-start.33
  492.9 1.3 collective-permute-start.32
  494.2 1.3 collective-permute-start.31
  495.5 1.4 collective-permute-start.30
  496.9 2.5 collective-permute-start.29
  499.5 1.9 collective-permute-start.28
  501.4 1.9 collective-permute-start.27
  503.3 2.2 collective-permute-start.26
  505.5 2.9 collective-permute-start.25
  508.3 2.8 collective-permute-start.24
  511.2 3.2 collective-permute-start.23
  514.4 3.1 collective-permute-start.22
  517.5 2.4 collective-permute-start.21
  520.0 3.5 collective-permute-start.20
  523.4 4.6 collective-permute-start.19
  528.1 4.6 collective-permute-start.18
  532.7 2.4 collective-permute-start.17
  535.2 3.4 collective-permute-start.16
  538.6 2.2 collective-permute-start.15
  540.9 3.9 collective-permute-start.14
  544.8 2.5 collective-permute-start.13
  547.3 2.2 collective-permute-start.12
  551.5 2.9 concatenate.77
  555.1 660.8 %all-reduce.5.cloned.1.call-done = f32[768,576]{0,1:T(8,128)} async-done(((f32[768,576]{0,1:T(8,128)}), f32[768,576]{0,1:T(8,128)}) %all-reduce.5.cloned.1.call-update) | async-done | bytes 1769488
  1215.9 1.2 constant_dynamic-slice_fusion.1
  (249 shorter events, 37.1 us)
Async XLA Ops:
  8.0 11.0 copy-start
  8.0 1207.9 %all-reduce.5.cloned.1.call-start = ((), (), s32[]{:S(2)}) async-start(), calls=%async_computation.2 | async-start | bytes 3538944
  8.8 26.9 %copy-start.36 = (pred[256]{0:T(512)(128)(4,1)}, pred[256]{0:T(512)(128)(4,1)S(1)}, u32[]{:S(2)}) copy-start(pred[256]{0:T(512)(128)(4,1)S(1)} %get-tuple-element.20) | copy-start | bytes 772
  9.9 76.1 %copy-start.26 = (pred[4,4]{0,1:T(4,128)(4,1)}, pred[4,4]{0,1:T(4,128)(4,1)S(1)}, u32[]{:S(2)}) copy-start(pred[4,4]{0,1:T(4,128)(4,1)S(1)} %iota_compare_fusion.1) | copy-start | bytes 52
  9.9 76.3 %copy-start.24 = (pred[16,4]{0,1:T(4,128)(4,1)}, pred[16,4]{0,1:T(4,128)(4,1)S(1)}, u32[]{:S(2)}) copy-start(pred[16,4]{0,1:T(4,128)(4,1)S(1)} %iota_compare_fusion) | copy-start | bytes 196
  10.1 27.5 %copy-start.33 = (bf16[64,4]{0,1:T(4,128)(2,1)}, bf16[64,4]{0,1:T(4,128)(2,1)S(1)}, u32[]{:S(2)}) copy-start(bf16[64,4]{0,1:T(4,128)(2,1)S(1)} %select_reduce_fusion.10) | copy-start | bytes 1540
  10.2 27.3 %collective-permute-start = (bf16[80,4]{0,1:T(4,128)(2,1)S(1)}, bf16[80,4]{0,1:T(4,128)(2,1)S(1)}, u32[]{:S(2)}, u32[]{:S(2)}) collective-permute-start(bf16[80,4]{0,1:T(4,128)(2,1)S(1)} %pad_maximum_fusion.11), channel_id=1, source_target_pairs={{0,4},{4,0},{8,12},{12,8},{16,20},{20,16},{24,28},{28,24},{32,36},... | collective-permute-start | bytes 1928 | tf_op jit(solution)/shard_map/ppermute | solution.py:18
  20.5 15.6 %copy-start.2 = (bf16[256,768]{1,0:T(8,128)(2,1)S(1)}, bf16[256,768]{1,0:T(8,128)(2,1)}, u32[]{:S(2)}) copy-start(bf16[256,768]{1,0:T(8,128)(2,1)} %param.11) | copy-start | bytes 1179652
  20.5 15.6 %copy-start.7 = (bf16[192,768]{1,0:T(8,128)(2,1)S(1)}, bf16[192,768]{1,0:T(8,128)(2,1)}, u32[]{:S(2)}) copy-start(bf16[192,768]{1,0:T(8,128)(2,1)} %param.10) | copy-start | bytes 884740
  23.0 35.4 %collective-permute-start.2 = (bf16[80,4,2,48]{0,3,1,2:T(8,128)(2,1)}, bf16[80,4,2,48]{0,3,1,2:T(8,128)(2,1)S(1)}, u32[]{:S(2)}, u32[]{:S(2)}) collective-permute-start(bf16[80,4,2,48]{0,3,1,2:T(8,128)(2,1)} %pad_maximum_fusion.6), channel_id=1, source_target_pairs={{0,4},{4,0},{8,12},{12,8},{16,20},{20,16},{24,28},{28,24},{32,36},... | collective-permute-start | bytes 184328 | tf_op jit(solution)/shard_map/ppermute | solution.py:18
  37.6 12.2 copy-start.35
  37.7 19.1 %copy-start.34 = (bf16[64,4]{0,1:T(4,128)(2,1)S(1)}, bf16[64,4]{0,1:T(4,128)(2,1)}, u32[]{:S(2)}) copy-start(bf16[64,4]{0,1:T(4,128)(2,1)} %copy-done.33) | copy-start | bytes 1540
  37.7 5.4 collective-permute-start.1
  43.3 6.7 collective-permute-start.4
  49.4 39.5 %copy-start.15 = (pred[256,4]{0,1:T(4,128)(4,1)}, pred[256,4]{0,1:T(4,128)(4,1)S(1)}, u32[]{:S(2)}) copy-start(pred[256,4]{0,1:T(4,128)(4,1)S(1)} %broadcast_in_dim.445) | copy-start | bytes 3076
  49.9 39.0 %copy-start.18 = (pred[256,4]{0,1:T(4,128)(4,1)}, pred[256,4]{0,1:T(4,128)(4,1)S(1)}, u32[]{:S(2)}) copy-start(pred[256,4]{0,1:T(4,128)(4,1)S(1)} %broadcast_in_dim.426) | copy-start | bytes 3076
  50.0 8.2 collective-permute-start.5
  57.6 31.0 %copy-start.28 = (pred[4,256]{1,0:T(4,128)(4,1)}, pred[4,256]{1,0:T(4,128)(4,1)S(1)}, u32[]{:S(2)}) copy-start(pred[4,256]{1,0:T(4,128)(4,1)S(1)} %compare_bitcast_fusion.1) | copy-start | bytes 3076
  58.6 6.4 collective-permute-start.3
  61.3 25.3 %copy-start.27 = (pred[4,256]{1,0:T(4,128)(4,1)}, pred[4,256]{1,0:T(4,128)(4,1)S(1)}, u32[]{:S(2)}) copy-start(pred[4,256]{1,0:T(4,128)(4,1)S(1)} %compare_bitcast_fusion) | copy-start | bytes 3076
  65.2 7.3 collective-permute-start.6
  72.5 7.7 copy-start.6
  73.3 16.3 %copy-start.37 = (pred[256]{0:T(512)(128)(4,1)S(1)}, pred[256]{0:T(512)(128)(4,1)}, u32[]{:S(2)}) copy-start(pred[256]{0:T(512)(128)(4,1)} %copy-done.36) | copy-start | bytes 772
  73.3 9.6 collective-permute-start.7
  89.8 7.3 copy-start.5
  107.4 9.4 collective-permute-start.8
  116.9 9.4 collective-permute-start.9
  122.0 7.3 copy-start.17
  127.3 7.5 collective-permute-start.10
  135.2 10.8 collective-permute-start.11
  150.1 1067.8 %reduce-scatter.5.cloned.1.call-start = ((), (), s32[]{:S(2)}) async-start(), calls=%async_computation.1 | async-start | bytes 491520 | tf_op jit(solution)/shard_map/reduce_scatter | solution.py:210
  150.1 399.4 %copy-start.39 = (u32[512]{0:T(512)S(1)}, u32[512]{0:T(512)}, u32[]{:S(2)}) copy-start(u32[512]{0:T(512)} %constant.28) | copy-start | bytes 6148
  461.5 7.8 collective-permute-start.42
  462.8 5.2 collective-permute-start.43
  464.1 6.5 collective-permute-start.41
  465.4 6.5 collective-permute-start.40
  466.7 6.5 collective-permute-start.39
  468.0 22.9 %collective-permute-start.38 = (f32[192,8]{0,1:T(8,128)S(1)}, f32[192,8]{0,1:T(8,128)S(1)}, u32[]{:S(2)}, u32[]{:S(2)}) collective-permute-start(f32[192,8]{0,1:T(8,128)S(1)} %fusion), channel_id=1, source_target_pairs={{0,108},{4,112},{8,116},{12,120},{16,124},{20,128},{24,132},{28,13... | collective-permute-start | bytes 18440
  469.3 23.6 %collective-permute-start.37 = (f32[192,8]{0,1:T(8,128)S(1)}, f32[192,8]{0,1:T(8,128)S(1)}, u32[]{:S(2)}, u32[]{:S(2)}) collective-permute-start(f32[192,8]{0,1:T(8,128)S(1)} %fusion), channel_id=1, source_target_pairs={{0,104},{4,108},{8,112},{12,116},{16,120},{20,124},{24,128},{28,13... | collective-permute-start | bytes 18440
  470.6 23.6 %collective-permute-start.36 = (f32[192,8]{0,1:T(8,128)S(1)}, f32[192,8]{0,1:T(8,128)S(1)}, u32[]{:S(2)}, u32[]{:S(2)}) collective-permute-start(f32[192,8]{0,1:T(8,128)S(1)} %fusion), channel_id=1, source_target_pairs={{0,100},{4,104},{8,108},{12,112},{16,116},{20,120},{24,124},{28,12... | collective-permute-start | bytes 18440
  471.9 23.6 %collective-permute-start.35 = (f32[192,8]{0,1:T(8,128)S(1)}, f32[192,8]{0,1:T(8,128)S(1)}, u32[]{:S(2)}, u32[]{:S(2)}) collective-permute-start(f32[192,8]{0,1:T(8,128)S(1)} %fusion), channel_id=1, source_target_pairs={{0,96},{4,100},{8,104},{12,108},{16,112},{20,116},{24,120},{28,124... | collective-permute-start | bytes 18440
  473.2 23.7 %collective-permute-start.34 = (f32[192,8]{0,1:T(8,128)S(1)}, f32[192,8]{0,1:T(8,128)S(1)}, u32[]{:S(2)}, u32[]{:S(2)}) collective-permute-start(f32[192,8]{0,1:T(8,128)S(1)} %fusion), channel_id=1, source_target_pairs={{0,92},{4,96},{8,100},{12,104},{16,108},{20,112},{24,116},{28,120}... | collective-permute-start | bytes 18440
  490.9 8.6 collective-permute-start.33
  492.9 8.5 collective-permute-start.32
  494.2 9.1 collective-permute-start.31
  495.5 10.0 collective-permute-start.30
  496.9 11.4 collective-permute-start.29
  499.5 11.7 collective-permute-start.28
  501.4 13.0 %collective-permute-start.27 = (f32[192,8]{0,1:T(8,128)S(1)}, f32[192,8]{0,1:T(8,128)S(1)}, u32[]{:S(2)}, u32[]{:S(2)}) collective-permute-start(f32[192,8]{0,1:T(8,128)S(1)} %fusion), channel_id=1, source_target_pairs={{0,64},{4,68},{8,72},{12,76},{16,80},{20,84},{24,88},{28,92},{32,9... | collective-permute-start | bytes 18440
  503.3 14.2 %collective-permute-start.26 = (f32[192,8]{0,1:T(8,128)S(1)}, f32[192,8]{0,1:T(8,128)S(1)}, u32[]{:S(2)}, u32[]{:S(2)}) collective-permute-start(f32[192,8]{0,1:T(8,128)S(1)} %fusion), channel_id=1, source_target_pairs={{0,60},{4,64},{8,68},{12,72},{16,76},{20,80},{24,84},{28,88},{32,9... | collective-permute-start | bytes 18440
  505.5 14.5 %collective-permute-start.25 = (f32[192,8]{0,1:T(8,128)S(1)}, f32[192,8]{0,1:T(8,128)S(1)}, u32[]{:S(2)}, u32[]{:S(2)}) collective-permute-start(f32[192,8]{0,1:T(8,128)S(1)} %fusion), channel_id=1, source_target_pairs={{0,56},{4,60},{8,64},{12,68},{16,72},{20,76},{24,80},{28,84},{32,8... | collective-permute-start | bytes 18440
  508.3 15.1 %collective-permute-start.24 = (f32[192,8]{0,1:T(8,128)S(1)}, f32[192,8]{0,1:T(8,128)S(1)}, u32[]{:S(2)}, u32[]{:S(2)}) collective-permute-start(f32[192,8]{0,1:T(8,128)S(1)} %fusion), channel_id=1, source_target_pairs={{0,52},{4,56},{8,60},{12,64},{16,68},{20,72},{24,76},{28,80},{32,8... | collective-permute-start | bytes 18440
  511.2 16.9 %collective-permute-start.23 = (f32[192,8]{0,1:T(8,128)S(1)}, f32[192,8]{0,1:T(8,128)S(1)}, u32[]{:S(2)}, u32[]{:S(2)}) collective-permute-start(f32[192,8]{0,1:T(8,128)S(1)} %fusion), channel_id=1, source_target_pairs={{0,48},{4,52},{8,56},{12,60},{16,64},{20,68},{24,72},{28,76},{32,8... | collective-permute-start | bytes 18440
  514.4 18.3 %collective-permute-start.22 = (f32[192,8]{0,1:T(8,128)S(1)}, f32[192,8]{0,1:T(8,128)S(1)}, u32[]{:S(2)}, u32[]{:S(2)}) collective-permute-start(f32[192,8]{0,1:T(8,128)S(1)} %fusion), channel_id=1, source_target_pairs={{0,44},{4,48},{8,52},{12,56},{16,60},{20,64},{24,68},{28,72},{32,7... | collective-permute-start | bytes 18440
  517.5 17.7 %collective-permute-start.21 = (f32[192,8]{0,1:T(8,128)S(1)}, f32[192,8]{0,1:T(8,128)S(1)}, u32[]{:S(2)}, u32[]{:S(2)}) collective-permute-start(f32[192,8]{0,1:T(8,128)S(1)} %fusion), channel_id=1, source_target_pairs={{0,40},{4,44},{8,48},{12,52},{16,56},{20,60},{24,64},{28,68},{32,7... | collective-permute-start | bytes 18440
  520.0 18.7 %collective-permute-start.20 = (f32[192,8]{0,1:T(8,128)S(1)}, f32[192,8]{0,1:T(8,128)S(1)}, u32[]{:S(2)}, u32[]{:S(2)}) collective-permute-start(f32[192,8]{0,1:T(8,128)S(1)} %fusion), channel_id=1, source_target_pairs={{0,36},{4,40},{8,44},{12,48},{16,52},{20,56},{24,60},{28,64},{32,6... | collective-permute-start | bytes 18440
  523.4 17.4 %collective-permute-start.19 = (f32[192,8]{0,1:T(8,128)S(1)}, f32[192,8]{0,1:T(8,128)S(1)}, u32[]{:S(2)}, u32[]{:S(2)}) collective-permute-start(f32[192,8]{0,1:T(8,128)S(1)} %fusion), channel_id=1, source_target_pairs={{0,32},{4,36},{8,40},{12,44},{16,48},{20,52},{24,56},{28,60},{32,6... | collective-permute-start | bytes 18440
  528.1 16.7 %collective-permute-start.18 = (f32[192,8]{0,1:T(8,128)S(1)}, f32[192,8]{0,1:T(8,128)S(1)}, u32[]{:S(2)}, u32[]{:S(2)}) collective-permute-start(f32[192,8]{0,1:T(8,128)S(1)} %fusion), channel_id=1, source_target_pairs={{0,28},{4,32},{8,36},{12,40},{16,44},{20,48},{24,52},{28,56},{32,6... | collective-permute-start | bytes 18440
  532.7 14.6 %collective-permute-start.17 = (f32[192,8]{0,1:T(8,128)S(1)}, f32[192,8]{0,1:T(8,128)S(1)}, u32[]{:S(2)}, u32[]{:S(2)}) collective-permute-start(f32[192,8]{0,1:T(8,128)S(1)} %fusion), channel_id=1, source_target_pairs={{0,24},{4,28},{8,32},{12,36},{16,40},{20,44},{24,48},{28,52},{32,5... | collective-permute-start | bytes 18440
  535.2 16.3 %collective-permute-start.16 = (f32[192,8]{0,1:T(8,128)S(1)}, f32[192,8]{0,1:T(8,128)S(1)}, u32[]{:S(2)}, u32[]{:S(2)}) collective-permute-start(f32[192,8]{0,1:T(8,128)S(1)} %fusion), channel_id=1, source_target_pairs={{0,20},{4,24},{8,28},{12,32},{16,36},{20,40},{24,44},{28,48},{32,5... | collective-permute-start | bytes 18440
  538.6 12.8 %collective-permute-start.15 = (f32[192,8]{0,1:T(8,128)S(1)}, f32[192,8]{0,1:T(8,128)S(1)}, u32[]{:S(2)}, u32[]{:S(2)}) collective-permute-start(f32[192,8]{0,1:T(8,128)S(1)} %fusion), channel_id=1, source_target_pairs={{0,16},{4,20},{8,24},{12,28},{16,32},{20,36},{24,40},{28,44},{32,4... | collective-permute-start | bytes 18440
  540.9 10.6 collective-permute-start.14
  544.8 6.7 collective-permute-start.13
  547.3 4.2 collective-permute-start.12
  (22 other events, 71.0 us)
Sparse Core Ops, SparseCore 0:
  150.2 1065.6 all-reduce.4
Sparse Core Ops, SparseCore 1:
  153.9 27.7 reduce-scatter.4
where the time goes:
time: 1230 us
  waiting for transfers between devices  681 us (55%)
  blocking collectives  310 us (25%)
  starting transfers between devices  162 us (13%)
  local copies, waits for them, and re-layouts  23.3 us (2%)
  between operations  18.4 us (1%)
  matrix products  17.2 us (1%)
  other arithmetic  13.7 us (1%)
    unnamed x35, waiting for transfers between devices  661 us
    unnamed x1, blocking collectives  310 us
    unnamed x33, starting transfers between devices  87.5 us
    ppermute x12, starting transfers between devices, swapped(): return lax.ppermute(block, axis, route)  74.3 us
  transfers between devices with their start and end apart: 46, of which 9 were waited for; matrix products, arithmetic and copies ran while one was open for 27% of the time, Pallas kernels for 0%

commit v1 on v0

v1 whole, which is shorter than its diff:
```python
import functools
import math

import jax
import jax.numpy as jnp
from jax import lax
from jax.experimental import pallas as pl
from jax.experimental.pallas import tpu as pltpu
from jax.sharding import PartitionSpec as P

BF = jnp.bfloat16
F32 = jnp.float32
MESH = pl.DeviceIdType.MESH

HEADS = 4
HD = 48
TOK = 256
D = 768
KV = 2 * HD * HEADS
QW = HD * HEADS
CORES = 2
ZN = 8
GROUP2 = 4
GROUP3 = 16
ROWS2 = TOK // GROUP2
ROWS3 = TOK // GROUP3
MARK = 2.0**100
MARK_TEST = 2.0**90
LOW = -1e30


def nn(a, b):
    return lax.dot_general(a, b, (((1,), (0,)), ((), ())), preferred_element_type=F32)


def nt(a, b):
    return lax.dot_general(a, b, (((1,), (1,)), ((), ())), preferred_element_type=F32)


def iota(shape, dim):
    return lax.broadcasted_iota(jnp.int32, shape, dim)


def one_hot(mask):
    return jnp.where(mask, 1.0, 0.0).astype(BF)


class Plan:
    def __init__(self, n_seq, n_head):
        self.n_seq = n_seq
        self.n_head = n_head
        self.yn = 2 if n_seq >= 32 else 1
        self.xn = n_seq // (CORES * ZN * self.yn)
        self.chips = n_seq // CORES
        self.rows_dev = D // n_seq
        self.rows_pad = -(-self.rows_dev // 8) * 8
        self.chunk = CORES * self.rows_pad
        self.rows = self.chips * self.chunk
        self.xrows = self.rows // self.xn
        self.zrows = self.xrows // ZN


def body(plan, offs, valid, tokens, wqkv, wout, ograd, gt_out, gw_out, go_out,
         proj, kv1, kv2, kv3, g2, g3, r2, r3, own, att_t, dq_t, dat_t, dat, tok_t, og_t,
         m, m_in, xs, xr, zs, zr, ys, yr, fin, pt, pr,
         a2s, a2r, a3s, a3r, b2s, b2r, b3s, b3r, cs, cr, ms, mr, xss, xrs, zss, zrs, yss, yrs):
    xn, yn, nh = plan.xn, plan.yn, plan.n_head
    factor = 1.0 / math.sqrt(HD)
    seq = lax.axis_index("seq")
    head = lax.axis_index("head")
    core = seq % CORES
    z = (seq // CORES) % ZN
    y = (seq // (CORES * ZN)) % yn
    x = seq // (CORES * ZN * yn)

    def place(xi, yi, zi, ci):
        return (((xi * yn + yi) * ZN + zi) * CORES + ci, head)

    pos3 = seq % GROUP3
    base3 = seq - pos3
    pos2 = seq % GROUP2
    base2 = seq - pos2
    other = 1 - core

    def peer3(d):
        return (base3 + (pos3 + d) % GROUP3, head)

    def peer2(d):
        return (base2 + (pos2 + d) % GROUP2, head)

    x_peers = [((x + d) % xn, d) for d in range(1, xn)]
    y_peers = [place(x, (y + 1) % yn, z, core), place(x, (y + 1) % yn, z, other)] if yn > 1 else []
    h_peers = [(seq, (head + d) % nh) for d in range(1, nh)]

    barrier = pltpu.get_barrier_semaphore()
    greeted = [peer3(d) for d in range(1, GROUP3)]
    greeted += [place(xi, y, z, core) for xi, _ in x_peers] + y_peers + h_peers
    for who in greeted:
        pl.semaphore_signal(barrier, inc=1, device_id=who, device_id_type=MESH)

    started = []

    def send(src, dst, ssem, rsem, who):
        copy = pltpu.make_async_remote_copy(
            src_ref=src, dst_ref=dst, send_sem=ssem, recv_sem=rsem,
            device_id=who, device_id_type=MESH)
        copy.start()
        started.append(copy)
        return copy

    proj[...] = nn(tokens[...], wqkv[...]).astype(BF)
    eye = iota((TOK, TOK), 0) == iota((TOK, TOK), 1)
    alive = jnp.sum(jnp.where(eye, valid[...].astype(F32), 0.0), axis=1, keepdims=True)
    packed = jnp.concatenate(
        [proj[:, 3 * HD * h + HD:3 * HD * (h + 1)] for h in range(HEADS)], axis=1)
    marked = (iota((TOK, KV), 1) % (2 * HD) == 0) & (alive == 0.0)
    kv1[...] = jnp.where(marked, MARK, packed.astype(F32)).astype(BF)
    for h in range(HEADS):
        rows = iota((ROWS2 + ROWS3, TOK), 0)
        want = jnp.where(rows < ROWS2, rows * GROUP2 + offs[h, 0],
                         (rows - ROWS2) * GROUP3 + offs[h, 1])
        pick = one_hot(iota((ROWS2 + ROWS3, TOK), 1) == want)
        cols = slice(2 * HD * h, 2 * HD * (h + 1))
        chosen = nn(pick, kv1[:, cols]).astype(BF)
        kv2[pos2, :, cols] = chosen[:ROWS2]
        kv3[pos3, :, cols] = chosen[ROWS2:]

    pl.semaphore_wait(barrier, len(greeted))
    a_copies = []
    for d in range(1, GROUP2):
        a_copies.append(send(kv2.at[pos2], kv2.at[pos2], a2s.at[d], a2r.at[d], peer2(d)))
    for d in range(1, GROUP3):
        a_copies.append(send(kv3.at[pos3], kv3.at[pos3], a3s.at[d], a3r.at[d], peer3(d)))

    dat[...] = nt(ograd[...], wout[...]).astype(BF)
    dat_t[...] = nt(wout[...], ograd[...]).astype(BF)
    half = plan.rows // 2
    rr = iota((half, 1), 0)
    spot = rr // plan.chunk
    inner = rr % plan.chunk
    y_of = spot % yn
    z_of = (spot // yn) % ZN
    x_of = spot // (yn * ZN)
    chip = (x_of * yn + y_of) * ZN + z_of
    j = inner % plan.rows_pad
    source = jnp.where(j < plan.rows_dev,
                       (chip * CORES + inner // plan.rows_pad) * plan.rows_dev + j, -1)
    place_rows = one_hot(iota((half, D // 2), 1) == source)
    for part in range(2):
        cols = slice(part * D // 2, (part + 1) * D // 2)
        to = slice(part * half, (part + 1) * half)
        tok_t[to] = nt(place_rows, tokens[:, cols]).astype(BF)
        og_t[to] = nt(place_rows, ograd[:, cols]).astype(BF)

    for copy in a_copies:
        copy.wait_recv()

    lane = iota((1, TOK), 1)
    eye_kv = one_hot(iota((KV, KV), 0) == iota((KV, KV), 1))
    keys = [kv1[...], kv2[...].reshape(TOK, KV), kv3[...].reshape(TOK, KV)]
    keys_t = [nt(eye_kv, k).astype(BF) for k in keys]
    for h in range(HEADS):
        kc = slice(2 * HD * h, 2 * HD * h + HD)
        vc = slice(2 * HD * h + HD, 2 * HD * (h + 1))
        hr = slice(HD * h, HD * (h + 1))
        q = proj[:, 3 * HD * h:3 * HD * h + HD]
        d = dat[:, hr]
        d_t = dat_t[hr, :]
        inside = [None, lane % GROUP2 == offs[h, 0], lane % GROUP3 == offs[h, 1]]
        scores = []
        top = None
        for level in range(3):
            k = keys[level][:, kc]
            keep = k[:, 0:1].astype(F32) < MARK_TEST
            if level:
                keep = keep & inside[level]
            s = jnp.where(keep, nt(k, q) * factor, LOW)
            peak = jnp.max(s, axis=0, keepdims=True)
            top = peak if top is None else jnp.maximum(top, peak)
            scores.append(s)
        weights = [jnp.exp(s - top) for s in scores]
        den = sum(jnp.sum(w, axis=0, keepdims=True) for w in weights)
        num = sum(nn(keys_t[level][vc, :], weights[level].astype(BF)) for level in range(3))
        inv = 1.0 / den
        att = (num * inv).astype(BF)
        att_t[hr, :] = att
        delta = jnp.sum(d_t.astype(F32) * att.astype(F32), axis=0, keepdims=True)
        dq = None
        for level in range(3):
            normed = weights[level] * inv
            v = keys[level][:, vc]
            ds = (normed * (nn(v, d_t) - delta)).astype(BF)
            dq_part = nn(keys_t[level][kc, :], ds)
            dq = dq_part if dq is None else dq + dq_part
            dk = nn(ds, q) * factor
            dv = nn(normed.astype(BF), d)
            if level == 0:
                own[:, kc] = dk
                own[:, vc] = dv
            elif level == 1:
                g2[:, :, kc] = dk.astype(BF).reshape(GROUP2, ROWS2, HD)
                g2[:, :, vc] = dv.astype(BF).reshape(GROUP2, ROWS2, HD)
            else:
                g3[:, :, kc] = dk.astype(BF).reshape(GROUP3, ROWS3, HD)
                g3[:, :, vc] = dv.astype(BF).reshape(GROUP3, ROWS3, HD)
        dq_t[hr, :] = (dq * factor).astype(BF)

    b_copies = []
    for d in range(1, GROUP2):
        b_copies.append(send(g2.at[(pos2 + d) % GROUP2], r2.at[pos2], b2s.at[d], b2r.at[d], peer2(d)))
    for d in range(1, GROUP3):
        b_copies.append(send(g3.at[(pos3 + d) % GROUP3], r3.at[pos3], b3s.at[d], b3r.at[d], peer3(d)))
    r2[pos2] = g2[pos2]
    r3[pos3] = g3[pos3]
    m[0, :, 0:QW] = nt(og_t[...], att_t[...]).astype(BF)
    m[0, :, QW:2 * QW] = nt(tok_t[...], dq_t[...]).astype(BF)
    for copy in b_copies:
        copy.wait_recv()

    parts = []
    for h in range(HEADS):
        cols = slice(2 * HD * h, 2 * HD * (h + 1))
        row, col = iota((TOK, TOK), 0), iota((TOK, TOK), 1)
        spread2 = one_hot(row == (col % ROWS2) * GROUP2 + offs[h, 0])
        spread3 = one_hot(row == (col % ROWS3) * GROUP3 + offs[h, 1])
        parts.append(own[:, cols]
                     + nn(spread2, r2[...].reshape(TOK, KV)[:, cols])
                     + nn(spread3, r3[...].reshape(TOK, KV)[:, cols]))
    dkv = jnp.concatenate(parts, axis=1).astype(BF)

    w = wqkv[...]
    wq = jnp.concatenate([w[:, 3 * HD * h:3 * HD * h + HD] for h in range(HEADS)], axis=1)
    wkv = jnp.concatenate([w[:, 3 * HD * h + HD:3 * HD * (h + 1)] for h in range(HEADS)], axis=1)
    pt[...] = (nn(wq, dq_t[...]) + nt(wkv, dkv)).astype(BF).reshape(pt.shape)
    c_copies = []
    for d in range(1, nh):
        to = (head + d) % nh
        c_copies.append(send(pt.at[to], pr.at[d], cs.at[d], cr.at[d], (seq, to)))

    m[1] = nn(tok_t[...], dkv).astype(BF)
    sibling = send(m.at[other], m_in, ms, mr, place(x, y, z, other))
    sibling.wait_recv()
    total = m[core].astype(F32) + m_in[...].astype(F32)
    xs[...] = total.astype(BF).reshape(xs.shape)
    x_copies = []
    for xi, d in x_peers:
        x_copies.append(send(xs.at[xi], xr.at[d], xss.at[d], xrs.at[d], place(xi, y, z, core)))
    total = xs[x].astype(F32)
    for copy, (_, d) in zip(x_copies, x_peers):
        copy.wait_recv()
        total = total + xr[d].astype(F32)
    zs[...] = total.astype(BF).reshape(zs.shape)
    z_copies = []
    for d in range(1, ZN):
        zi = (z + d) % ZN
        z_copies.append(send(zs.at[zi], zr.at[d], zss.at[d], zrs.at[d], place(x, y, zi, core)))
    total = zs[z].astype(F32)
    for d in range(1, ZN):
        z_copies[d - 1].wait_recv()
        total = total + zr[d].astype(F32)
    ys[...] = total.astype(BF).reshape(ys.shape)
    far = (y + 1) % yn
    y_copies = [send(ys.at[y], yr.at[0], yss.at[0], yrs.at[0], place(x, y, z, other))]
    if yn > 1:
        y_copies.append(send(ys.at[far], yr.at[1], yss.at[1], yrs.at[1], y_peers[0]))
        y_copies.append(send(ys.at[far], yr.at[2], yss.at[2], yrs.at[2], y_peers[1]))

    total = pt[head].astype(F32)
    for d in range(1, nh):
        c_copies[d - 1].wait_recv()
        total = total + pr[d].astype(F32)
    eye_b = one_hot(eye)
    gt_out[...] = nt(eye_b, total.astype(BF)).astype(BF)

    for copy in y_copies:
        copy.wait_recv()
    mine = ys[y].astype(F32)
    theirs = yr[0].astype(F32)
    if yn > 1:
        mine = mine + yr[1].astype(F32)
        theirs = theirs + yr[2].astype(F32)
    fin[core] = mine
    fin[other] = theirs
    rows = pl.ds(pl.multiple_of(core * plan.rows_pad, 8), plan.rows_pad)
    first = fin[0, rows, :][:plan.rows_dev]
    second = fin[1, rows, :][:plan.rows_dev]
    go_out[...] = first[:, :QW]
    gw_out[...] = jnp.concatenate(
        [piece for h in range(HEADS)
         for piece in (first[:, QW + HD * h:QW + HD * (h + 1)],
                       second[:, 2 * HD * h:2 * HD * (h + 1)])], axis=1)
    for copy in started:
        copy.wait_send()


def per_device(plan, tokens, valid, offsets, qkv_weight, out_weight, out_grad):
    vm = pl.BlockSpec(memory_space=pltpu.VMEM)
    sm = pl.BlockSpec(memory_space=pltpu.SMEM)
    dma = pltpu.SemaphoreType.DMA
    nh, xn, yn, rows = plan.n_head, plan.xn, plan.yn, plan.rows
    scratch = [
        pltpu.VMEM((TOK, 3 * QW), BF),
        pltpu.VMEM((TOK, KV), BF),
        pltpu.VMEM((GROUP2, ROWS2, KV), BF),
        pltpu.VMEM((GROUP3, ROWS3, KV), BF),
        pltpu.VMEM((GROUP2, ROWS2, KV), BF),
        pltpu.VMEM((GROUP3, ROWS3, KV), BF),
        pltpu.VMEM((GROUP2, ROWS2, KV), BF),
        pltpu.VMEM((GROUP3, ROWS3, KV), BF),
        pltpu.VMEM((TOK, KV), F32),
        pltpu.VMEM((QW, TOK), BF),
        pltpu.VMEM((QW, TOK), BF),
        pltpu.VMEM((QW, TOK), BF),
        pltpu.VMEM((TOK, QW), BF),
        pltpu.VMEM((rows, TOK), BF),
        pltpu.VMEM((rows, TOK), BF),
        pltpu.VMEM((2, rows, KV), BF),
        pltpu.VMEM((rows, KV), BF),
        pltpu.VMEM((xn, plan.xrows, KV), BF),
        pltpu.VMEM((xn, plan.xrows, KV), BF),
        pltpu.VMEM((ZN, plan.zrows, KV), BF),
        pltpu.VMEM((ZN, plan.zrows, KV), BF),
        pltpu.VMEM((yn, plan.chunk, KV), BF),
        pltpu.VMEM((3, plan.chunk, KV), BF),
        pltpu.VMEM((2, plan.chunk, KV), F32),
        pltpu.VMEM((4, D // 4, TOK), BF),
        pltpu.VMEM((4, D // 4, TOK), BF),
        dma((GROUP2,)), dma((GROUP2,)), dma((GROUP3,)), dma((GROUP3,)),
        dma((GROUP2,)), dma((GROUP2,)), dma((GROUP3,)), dma((GROUP3,)),
        dma((4,)), dma((4,)), dma, dma,
        dma((4,)), dma((4,)), dma((ZN,)), dma((ZN,)), dma((3,)), dma((3,)),
    ]
    gt, gw, go = pl.pallas_call(
        functools.partial(body, plan),
        out_shape=(
            jax.ShapeDtypeStruct((TOK, D // 4), BF),
            jax.ShapeDtypeStruct((plan.rows_dev, 3 * QW), F32),
            jax.ShapeDtypeStruct((plan.rows_dev, QW), F32),
        ),
        in_specs=[sm] + [vm] * 5,
        out_specs=(vm, vm, vm),
        scratch_shapes=scratch,
        compiler_params=pltpu.CompilerParams(
            collective_id=0, has_side_effects=True, vmem_limit_bytes=48 * 1024 * 1024),
        cost_estimate=pl.CostEstimate(flops=2_000_000_000, bytes_accessed=4_000_000,
                                      transcendentals=800_000),
    )(offsets, valid.reshape(1, TOK), tokens, qkv_weight, out_weight, out_grad)
    return gt, gw, go.T


def solution(mesh):
    plan = Plan(mesh.shape["seq"], mesh.shape["head"])
    return jax.shard_map(
        functools.partial(per_device, plan),
        mesh=mesh,
        in_specs=(
            P("seq", None),
            P("seq"),
            P("head", None),
            P(None, "head"),
            P("head", None),
            P("seq", None),
        ),
        out_specs=(P("seq", "head"), P("seq", "head"), P("head", "seq")),
        check_vma=False,
    )
```

time: 1230 us -> 72.2 us (0.06)
  waiting for transfers between devices: 681 us -> 0 us
  blocking collectives: 310 us -> 0 us
  starting transfers between devices: 162 us -> 0 us
  Pallas kernels: 0 us -> 67 us
  local copies, waits for them, and re-layouts: 23.3 us -> 4.35 us
  between operations: 18.4 us -> 0.69 us
  matrix products: 17.2 us -> 0 us
  other arithmetic: 13.7 us -> 0 us
    unnamed x35 -> x0, waiting for transfers between devices: 661 us -> none
    unnamed x1 -> x0, blocking collectives: 310 us -> none
    unnamed x33 -> x0, starting transfers between devices: 87.5 us -> none
    ppermute x12 -> x0, starting transfers between devices: 74.3 us -> none  [swapped(): return lax.ppermute(block, axis, route)]
    pallas_call x0 -> x1, Pallas kernels: none -> 67 us  [per_device(): pl.pallas_call(functools.partial(body, plan), out_shape=(jax.ShapeDtypeSt...]
    ppermute x12 -> x0, waiting for transfers between devices: 20.2 us -> none  [swapped(): return lax.ppermute(block, axis, route)]
    dot_general x23 -> x0, matrix products: 17.2 us -> none  [the longest x3 2.93 us: per_device(): jnp.einsum('tqs,tqg->sqg', normalized_scores.astype(jnp.bfloat16), select...]
  transfers between devices with their start and end apart: 46 -> 0, of which waited for: 9 -> 0; matrix products, arithmetic and copies ran while one was open for 27% -> 0% of each run, Pallas kernels for 0% -> 0%
where the time goes in v1:
time: 72.2 us; the launch traced here: 72.1 us
  Pallas kernels  67 us (93%)
  local copies, waits for them, and re-layouts  4.35 us (6%)
    pallas_call x1, Pallas kernels, per_device(): pl.pallas_call(functools.partial(body, plan), out_shape=(jax.ShapeDtypeSt...  67 us
    unnamed x15, local copies, waits for them, and re-layouts  4.35 us

profile of v1, /device:TPU:1, one launch (start us, length us, event | category | flops | bytes accessed | tf_op | source)
XLA Modules:
  0.0 72.1 jit_solution(17081045197757370857)
XLA Ops:
  0.6 0.0 copy-start.4
  0.6 0.7 copy-done.4
  1.3 0.1 copy.9.offs
  1.4 0.0 copy-start
  1.4 0.0 copy-start.1
  1.4 0.0 copy-start.2
  1.4 0.0 copy-start.3
  1.4 1.6 %copy.10.wqkv = bf16[768,576]{1,0:T(8,128)(2,1)S(1)} copy(bf16[768,576]{0,1:T(8,128)(2,1)} %param.9) | data formatting | bytes 1769472 | tf_op args[3]
  3.0 0.0 copy-done
  3.1 0.0 copy-done.1
  3.1 0.0 copy-done.2
  3.1 0.0 copy-done.3
  3.1 67.0 %shard_map.85 = (bf16[256,192]{1,0:T(8,128)(2,1)S(1)}, f32[6,576]{1,0:T(8,128)S(1)}, f32[6,192]{1,0:T(8,128)S(1)}) custom-call(s32[4,2]{1,0:T(4,128)S(1)} %copy.9.offs, s32[1,256]{1,0:T(1,128)S(1)} %bitcast.3, bf16[256,768]{1,0:T(8,128)(2,1)S(1)} %copy-done, bf16[768,576]{1,0:T(8,128)(2,1)S(1)} %copy.10.wqkv, bf16[192,768]{1,0:T(8,128)(2,1)S(1)} %copy-done.2, ...), custom_call_target="tpu_custom_call" | custom-call | flops 2000000000 | bytes 4000000 | tf_op jit(solution)/shard_map/pallas_call | solution.py:333
  70.1 0.7 %copy.11 = bf16[256,192]{0,1:T(8,128)(2,1)} copy(bf16[256,192]{1,0:T(8,128)(2,1)S(1)} %get-tuple-element.9) | data formatting | bytes 196608
  70.9 0.6 copy.14
  71.5 0.6 copy.15
Async XLA Ops:
  0.6 0.7 copy-start.4
  1.4 1.6 %copy-start = (bf16[256,768]{1,0:T(8,128)(2,1)S(1)}, bf16[256,768]{1,0:T(8,128)(2,1)}, u32[]{:S(2)}) copy-start(bf16[256,768]{1,0:T(8,128)(2,1)} %tokens.1) | copy-start | bytes 1179652
  1.4 1.7 %copy-start.1 = (bf16[256,768]{1,0:T(8,128)(2,1)S(1)}, bf16[256,768]{1,0:T(8,128)(2,1)}, u32[]{:S(2)}) copy-start(bf16[256,768]{1,0:T(8,128)(2,1)} %ograd.1) | copy-start | bytes 1179652
  1.4 1.7 %copy-start.2 = (bf16[192,768]{1,0:T(8,128)(2,1)S(1)}, bf16[192,768]{1,0:T(8,128)(2,1)}, u32[]{:S(2)}) copy-start(bf16[192,768]{1,0:T(8,128)(2,1)} %wout.1) | copy-start | bytes 884740
  1.4 1.7 %copy-start.3 = (s32[256]{0:T(256)S(1)}, s32[256]{0:T(256)}, u32[]{:S(2)}) copy-start(s32[256]{0:T(256)} %param.7) | copy-start | bytes 3076

commit v2 on v1

v2 whole, which is shorter than its diff:
```python
import functools
import math

import jax
import jax.numpy as jnp
from jax import lax
from jax.experimental import pallas as pl
from jax.experimental.pallas import tpu as pltpu
from jax.sharding import PartitionSpec as P

BF = jnp.bfloat16
F32 = jnp.float32
MESH = pl.DeviceIdType.MESH

HEADS = 4
HD = 48
TOK = 256
D = 768
CORES = 2
MINE = HEADS // CORES
KV = 2 * HD * MINE
QW = HD * MINE
ALL = KV + QW
PAY = CORES * KV
ZN = 8
PAIR = 2
SPAN2 = 4
SPAN3 = 16
ROWS2 = TOK // SPAN2
ROWS3 = TOK // SPAN3
MARK = 2.0**100
MARK_TEST = 2.0**90
LOW = -1e30


def nn(a, b):
    return lax.dot_general(a, b, (((1,), (0,)), ((), ())), preferred_element_type=F32)


def nt(a, b):
    return lax.dot_general(a, b, (((1,), (1,)), ((), ())), preferred_element_type=F32)


def iota(shape, dim):
    return lax.broadcasted_iota(jnp.int32, shape, dim)


def one_hot(mask):
    return jnp.where(mask, 1.0, 0.0).astype(BF)


class Plan:
    def __init__(self, n_seq, n_head):
        self.n_head = n_head
        self.yn = 2 if n_seq >= 32 else 1
        self.xn = n_seq // (CORES * ZN * self.yn)
        self.rows_dev = D // n_seq
        self.rows_pad = -(-self.rows_dev // 8) * 8
        self.chunk = CORES * self.rows_pad
        self.rows = (n_seq // CORES) * self.chunk
        self.xrows = ZN * self.chunk
        self.lanes = self.yn * KV


def body(plan, offs, valid, tokens, wqkv, wout, ograd, gt_out, gw_out, go_out,
         p_out, tok_in, og_in, proj, kv2, kv3, g2, g3, r2, r3, own, att_t, dq_t,
         dat_t, tok_t, og_t, wn, d_out, d_in, q_out, q_in,
         xs, xr, zs, zr, ys, yr, fin, pt, pr,
         es, er, a2s, a2r, a3s, a3r, b2s, b2r, b3s, b3r, ds_, dr_, cs, cr,
         xss, xrs, zss, zrs, yss, yrs):
    xn, yn, nh = plan.xn, plan.yn, plan.n_head
    factor = 1.0 / math.sqrt(HD)
    seq = lax.axis_index("seq")
    head = lax.axis_index("head")
    core = seq % CORES
    other = 1 - core
    z = (seq // CORES) % ZN
    y = (seq // (CORES * ZN)) % yn
    x = seq // (CORES * ZN * yn)

    def place(xi, yi, zi, ci):
        return (((xi * yn + yi) * ZN + zi) * CORES + ci, head)

    pos2 = z % PAIR
    mate = z - pos2 + 1 - pos2
    sibling = place(x, y, z, other)
    z_peers = [(z + d) % ZN for d in range(1, ZN)]
    x_peers = [(x + d) % xn for d in range(1, xn)]
    far = (y + 1) % yn
    y_peers = [sibling]
    if yn > 1:
        y_peers += [place(x, far, z, core), place(x, far, z, other)]

    barrier = pltpu.get_barrier_semaphore()
    greeted = y_peers + [place(x, y, zi, core) for zi in z_peers]
    greeted += [place(xi, y, z, core) for xi in x_peers]
    greeted += [(seq, (head + d) % nh) for d in range(1, nh)]
    for who in greeted:
        pl.semaphore_signal(barrier, inc=1, device_id=who, device_id_type=MESH)

    started = []

    def send(src, dst, ssem, rsem, who):
        copy = pltpu.make_async_remote_copy(
            src_ref=src, dst_ref=dst, send_sem=ssem, recv_sem=rsem,
            device_id=who, device_id_type=MESH)
        copy.start()
        started.append(copy)
        return copy

    def heads_of(c):
        base = c * (MINE * 3 * HD)
        rows = [wqkv[pl.ds(pl.multiple_of(base + 3 * HD * h + HD, 16), 2 * HD), :]
                for h in range(MINE)]
        rows += [wqkv[pl.ds(pl.multiple_of(base + 3 * HD * h, 16), HD), :]
                 for h in range(MINE)]
        return (jnp.concatenate(rows, axis=0),
                wout[pl.ds(pl.multiple_of(c * QW, 16), QW), :])

    eye = iota((TOK, TOK), 0) == iota((TOK, TOK), 1)
    eye_b = one_hot(eye)
    alive = jnp.sum(jnp.where(eye, valid[...].astype(F32), 0.0), axis=1, keepdims=True)
    lane = iota((TOK, ALL), 1)
    marked = (lane % (2 * HD) == 0) & (lane < KV) & (alive == 0.0)

    def project(to, weights):
        to[:, :ALL] = jnp.where(marked, MARK, nt(tokens[...], weights[0])).astype(BF)
        to[:, ALL:] = nt(ograd[...], weights[1]).astype(BF)

    w_other = heads_of(other)
    project(p_out, w_other)
    pl.semaphore_wait(barrier, len(greeted))
    swap = send(p_out, proj.at[1], es.at[0], er.at[0], sibling)

    w_mine = heads_of(core)
    project(proj.at[0], w_mine)
    phase2 = [offs[0, core * MINE + h] for h in range(MINE)]
    phase3 = [offs[1, core * MINE + h] for h in range(MINE)]
    picks = []
    for h in range(MINE):
        rows = iota((ROWS2 + ROWS3, TOK), 0)
        want = jnp.where(rows < ROWS2, rows * SPAN2 + phase2[h],
                         (rows - ROWS2) * SPAN3 + phase3[h])
        picks.append(one_hot(iota((ROWS2 + ROWS3, TOK), 1) == want))

    def choose(b):
        for h in range(MINE):
            chosen = nn(picks[h], proj[b, :, 2 * HD * h:2 * HD * (h + 1)]).astype(BF)
            cols = slice(b * KV + 2 * HD * h, b * KV + 2 * HD * (h + 1))
            kv2[pos2, :, cols] = chosen[:ROWS2]
            kv3[z, :, cols] = chosen[ROWS2:]

    choose(0)
    swap.wait_recv()
    choose(1)

    a_copies = [send(kv2.at[pos2], kv2.at[pos2], a2s, a2r, place(x, y, mate, core))]
    for d, zi in enumerate(z_peers):
        a_copies.append(send(kv3.at[z], kv3.at[z], a3s.at[d], a3r.at[d], place(x, y, zi, core)))

    tok_swap = send(tokens, tok_in, es.at[1], er.at[1], sibling)
    og_swap = send(ograd, og_in, es.at[2], er.at[2], sibling)

    dat_t[:, :TOK] = nt(w_mine[1], ograd[...]).astype(BF)
    dat_t[:, TOK:] = nt(eye_b[:QW, :QW], proj[1, :, ALL:]).astype(BF)
    half = plan.rows // 2
    rr = iota((half, 1), 0)
    inner = rr % plan.chunk
    j = inner % plan.rows_pad
    source = jnp.where(
        j < plan.rows_dev,
        ((rr // plan.chunk) * CORES + inner // plan.rows_pad) * plan.rows_dev + j, -1)
    place_rows = one_hot(iota((half, D // 2), 1) == source)

    def place_block(to, block, b):
        for part in range(2):
            cols = slice(part * D // 2, (part + 1) * D // 2)
            to[part * half:(part + 1) * half, b * TOK:(b + 1) * TOK] = nt(
                place_rows, block[:, cols]).astype(BF)

    place_block(tok_t, tokens, 0)
    place_block(og_t, ograd, 0)
    eye_d = one_hot(iota((D, D), 0) == iota((D, D), 1))
    wn[0] = nt(eye_d, w_mine[0]).astype(BF)
    wn[1] = nt(eye_d, w_other[0]).astype(BF)

    for copy in a_copies:
        copy.wait_recv()

    lane = iota((1, TOK), 1)
    eye_kv = one_hot(iota((PAY, PAY), 0) == iota((PAY, PAY), 1))
    near, wide = kv2[...].reshape(PAIR * ROWS2, PAY), kv3[...].reshape(ZN * ROWS3, PAY)
    near_t, wide_t = nt(eye_kv, near).astype(BF), nt(eye_kv, wide).astype(BF)
    local_t = [nt(eye_kv[:KV, :KV], proj[b, :, :KV]).astype(BF) for b in range(2)]
    far_grads = {}
    for h in range(MINE):
        lo, mid, hi = 2 * HD * h, 2 * HD * h + HD, 2 * HD * (h + 1)
        hr = slice(HD * h, HD * (h + 1))
        keys, values, keys_t, values_t = {}, {}, {}, {}
        for level, rows, cols in ((1, near, near_t), (2, wide, wide_t)):
            keys[level] = jnp.concatenate([rows[:, lo:mid], rows[:, KV + lo:KV + mid]], axis=0)
            values[level] = jnp.concatenate([rows[:, mid:hi], rows[:, KV + mid:KV + hi]], axis=0)
            keys_t[level] = jnp.concatenate([cols[lo:mid], cols[KV + lo:KV + mid]], axis=1)
            values_t[level] = jnp.concatenate([cols[mid:hi], cols[KV + mid:KV + hi]], axis=1)
        inside = [None, lane % SPAN2 == phase2[h], lane % SPAN3 == phase3[h]]
        for b in range(2):
            at = slice(b * TOK, (b + 1) * TOK)
            keys[0], values[0] = proj[b, :, lo:mid], proj[b, :, mid:hi]
            keys_t[0], values_t[0] = local_t[b][lo:mid], local_t[b][mid:hi]
            q = proj[b, :, KV + HD * h:KV + HD * (h + 1)]
            d = proj[b, :, ALL + HD * h:ALL + HD * (h + 1)]
            d_t = dat_t[hr, at]
            scores = []
            top = None
            for level in range(3):
                k = keys[level]
                keep = k[:, 0:1].astype(F32) < MARK_TEST
                if level:
                    keep = keep & inside[level]
                s = jnp.where(keep, nt(k, q) * factor, LOW)
                peak = jnp.max(s, axis=0, keepdims=True)
                top = peak if top is None else jnp.maximum(top, peak)
                scores.append(s)
            weights = [jnp.exp(s - top) for s in scores]
            den = sum(jnp.sum(w, axis=0, keepdims=True) for w in weights)
            num = sum(nn(values_t[level], weights[level].astype(BF)) for level in range(3))
            inv = 1.0 / den
            att = (num * inv).astype(BF)
            att_t[hr, at] = att
            delta = jnp.sum(d_t.astype(F32) * att.astype(F32), axis=0, keepdims=True)
            dq = None
            for level in range(3):
                normed = weights[level] * inv
                grad = (normed * (nn(values[level], d_t) - delta)).astype(BF)
                dq_part = nn(keys_t[level], grad)
                dq = dq_part if dq is None else dq + dq_part
                dk = nn(grad, q) * factor
                dv = nn(normed.astype(BF), d)
                if level == 0:
                    own[b, :, lo:mid] = dk
                    own[b, :, mid:hi] = dv
                elif b == 0:
                    far_grads[level] = (dk, dv)
                else:
                    dk, dv = dk + far_grads[level][0], dv + far_grads[level][1]
                    to, n = (g2, PAIR) if level == 1 else (g3, ZN)
                    for part in range(2):
                        pick = slice(part * 2 * TOK // 4, (part + 1) * 2 * TOK // 4)
                        put = part * KV
                        to[:, :, put + lo:put + mid] = dk[pick].astype(BF).reshape(n, -1, HD)
                        to[:, :, put + mid:put + hi] = dv[pick].astype(BF).reshape(n, -1, HD)
            dq_t[hr, at] = (dq * factor).astype(BF)

    b_copies = [send(g2.at[1 - pos2], r2.at[pos2], b2s, b2r, place(x, y, mate, core))]
    for d, zi in enumerate(z_peers):
        b_copies.append(send(g3.at[zi], r3.at[z], b3s.at[d], b3r.at[d], place(x, y, zi, core)))
    r2[pos2] = g2[pos2]
    r3[z] = g3[z]

    def pack(i, col, block):
        width = block.shape[1]
        block = block.astype(BF).reshape(xn, yn, plan.xrows, width)
        for yi in range(yn):
            xs[i, :, :, yi * KV + col:yi * KV + col + width] = block[:, yi]

    def start_x(i):
        return [send(xs.at[i, xi], xr.at[i, d], xss.at[i, d], xrs.at[i, d], place(xi, y, z, core))
                for d, xi in enumerate(x_peers)]

    def start_z(i, copies):
        total = xs[i, x].astype(F32)
        for d, copy in enumerate(copies):
            copy.wait_recv()
            total = total + xr[i, d].astype(F32)
        zs[i] = total.astype(BF).reshape(ZN, plan.chunk, plan.lanes)
        return [send(zs.at[i, zi], zr.at[i, d], zss.at[i, d], zrs.at[i, d], place(x, y, zi, core))
                for d, zi in enumerate(z_peers)]

    def start_y(i, copies):
        total = zs[i, z].astype(F32)
        for d, copy in enumerate(copies):
            copy.wait_recv()
            total = total + zr[i, d].astype(F32)
        ys[i] = total.astype(BF)
        return [send(ys.at[i], yr.at[d, i], yss.at[d, i], yrs.at[d, i], who)
                for d, who in enumerate(y_peers)]

    dq = [nt(eye_b, dq_t[:, b * TOK:(b + 1) * TOK]).astype(BF) for b in range(2)]
    q_out[...] = dq[1]
    q_swap = send(q_out, q_in, ds_.at[0], dr_.at[0], sibling)
    og_swap.wait_recv()
    place_block(og_t, og_in, 1)
    pack(0, 0, nt(og_t[...], att_t[...]))
    tok_swap.wait_recv()
    place_block(tok_t, tok_in, 1)
    pack(0, QW, nt(tok_t[...], dq_t[...]))
    x_first = start_x(0)
    spreads = []
    for h in range(MINE):
        row, col = iota((TOK, TOK), 0), iota((TOK, TOK), 1)
        spreads.append(one_hot(row == jnp.where(
            col < PAIR * ROWS2, (col % ROWS2) * SPAN2 + phase2[h],
            (col % ROWS3) * SPAN3 + phase3[h])))
    for copy in b_copies:
        copy.wait_recv()
    back = jnp.concatenate([r2[...].reshape(PAIR * ROWS2, PAY),
                            r3[...].reshape(ZN * ROWS3, PAY)], axis=0)
    dkv = []
    for b in range(2):
        parts = []
        for h in range(MINE):
            cols = slice(2 * HD * h, 2 * HD * (h + 1))
            got = slice(b * KV + 2 * HD * h, b * KV + 2 * HD * (h + 1))
            parts.append(own[b, :, cols] + nn(spreads[h], back[:, got]))
        dkv.append(jnp.concatenate(parts, axis=1).astype(BF))
    d_out[...] = dkv[1]
    swap = send(d_out, d_in, ds_.at[1], dr_.at[1], sibling)
    pack(1, 0, nn(tok_t[...], jnp.concatenate(dkv, axis=0)))
    x_second = start_x(1)

    shares = nt(wn[0], jnp.concatenate([dkv[0], dq[0]], axis=1))
    q_swap.wait_recv()
    swap.wait_recv()
    shares = shares + nt(wn[1], jnp.concatenate([d_in[...], q_in[...]], axis=1))
    pt[...] = shares.astype(BF).reshape(pt.shape)
    c_copies = []
    for d in range(1, nh):
        to = (head + d) % nh
        c_copies.append(send(pt.at[to], pr.at[d], cs.at[d], cr.at[d], (seq, to)))

    z_first = start_z(0, x_first)
    z_second = start_z(1, x_second)
    y_first = start_y(0, z_first)
    y_second = start_y(1, z_second)

    total = pt[head].astype(F32)
    for d in range(1, nh):
        c_copies[d - 1].wait_recv()
        total = total + pr[d].astype(F32)
    gt_out[...] = total.astype(BF)

    for i, copies in enumerate((y_first, y_second)):
        for copy in copies:
            copy.wait_recv()
        mine = ys[i].astype(F32)
        theirs = yr[0, i].astype(F32)
        if yn > 1:
            mine = mine + yr[1, i].astype(F32)
            theirs = theirs + yr[2, i].astype(F32)
            mine = jnp.where(y == 0, mine[:, :KV], mine[:, KV:])
            theirs = jnp.where(y == 0, theirs[:, :KV], theirs[:, KV:])
        fin[core, :, i * KV:(i + 1) * KV] = mine
        fin[other, :, i * KV:(i + 1) * KV] = theirs
    rows = pl.ds(pl.multiple_of(core * plan.rows_pad, 8), plan.rows_pad)
    done = [fin[c, rows, :][:plan.rows_dev] for c in range(CORES)]
    go_out[...] = jnp.concatenate([f[:, :QW] for f in done], axis=1)
    gw_out[...] = jnp.concatenate(
        [piece for f in done for h in range(MINE)
         for piece in (f[:, QW + HD * h:QW + HD * (h + 1)],
                       f[:, KV + 2 * HD * h:KV + 2 * HD * (h + 1)])], axis=1)
    for copy in started:
        copy.wait_send()


def per_device(plan, tokens, valid, offsets, qkv_weight, out_weight, out_grad):
    vm = pl.BlockSpec(memory_space=pltpu.VMEM)
    sm = pl.BlockSpec(memory_space=pltpu.SMEM)
    dma = pltpu.SemaphoreType.DMA
    xn, rows, lanes = plan.xn, plan.rows, plan.lanes
    near, wide = pltpu.VMEM((PAIR, ROWS2, PAY), BF), pltpu.VMEM((ZN, ROWS3, PAY), BF)
    scratch = [
        pltpu.VMEM((TOK, ALL + QW), BF),
        pltpu.VMEM((TOK, D), BF),
        pltpu.VMEM((TOK, D), BF),
        pltpu.VMEM((2, TOK, ALL + QW), BF),
        near, wide, near, wide, near, wide,
        pltpu.VMEM((2, TOK, KV), F32),
        pltpu.VMEM((QW, 2 * TOK), BF),
        pltpu.VMEM((QW, 2 * TOK), BF),
        pltpu.VMEM((QW, 2 * TOK), BF),
        pltpu.VMEM((rows, 2 * TOK), BF),
        pltpu.VMEM((rows, 2 * TOK), BF),
        pltpu.VMEM((2, D, ALL), BF),
        pltpu.VMEM((TOK, KV), BF),
        pltpu.VMEM((TOK, KV), BF),
        pltpu.VMEM((TOK, QW), BF),
        pltpu.VMEM((TOK, QW), BF),
        pltpu.VMEM((2, xn, plan.xrows, lanes), BF),
        pltpu.VMEM((2, xn, plan.xrows, lanes), BF),
        pltpu.VMEM((2, ZN, plan.chunk, lanes), BF),
        pltpu.VMEM((2, ZN, plan.chunk, lanes), BF),
        pltpu.VMEM((2, plan.chunk, lanes), BF),
        pltpu.VMEM((3, 2, plan.chunk, lanes), BF),
        pltpu.VMEM((2, plan.chunk, 2 * KV), F32),
        pltpu.VMEM((4, D // 4, TOK), BF),
        pltpu.VMEM((4, D // 4, TOK), BF),
        dma((3,)), dma((3,)), dma, dma, dma((ZN,)), dma((ZN,)),
        dma, dma, dma((ZN,)), dma((ZN,)), dma((2,)), dma((2,)), dma((4,)), dma((4,)),
        dma((2, 4)), dma((2, 4)), dma((2, ZN)), dma((2, ZN)), dma((3, 2)), dma((3, 2)),
    ]
    gt, gw, go = pl.pallas_call(
        functools.partial(body, plan),
        out_shape=(
            jax.ShapeDtypeStruct((D // 4, TOK), BF),
            jax.ShapeDtypeStruct((plan.rows_dev, HEADS * 3 * HD), F32),
            jax.ShapeDtypeStruct((plan.rows_dev, HEADS * HD), F32),
        ),
        in_specs=[sm] + [vm] * 5,
        out_specs=(vm, vm, vm),
        scratch_shapes=scratch,
        compiler_params=pltpu.CompilerParams(
            collective_id=0, has_side_effects=True, vmem_limit_bytes=48 * 1024 * 1024),
        cost_estimate=pl.CostEstimate(flops=2_000_000_000, bytes_accessed=4_000_000,
                                      transcendentals=800_000),
    )(offsets.T, valid.reshape(1, TOK), tokens, qkv_weight.T, out_weight, out_grad)
    return gt.T, gw, go.T


def solution(mesh):
    plan = Plan(mesh.shape["seq"], mesh.shape["head"])
    return jax.shard_map(
        functools.partial(per_device, plan),
        mesh=mesh,
        in_specs=(
            P("seq", None),
            P("seq"),
            P("head", None),
            P(None, "head"),
            P("head", None),
            P("seq", None),
        ),
        out_specs=(P("seq", "head"), P("seq", "head"), P("head", "seq")),
        check_vma=False,
    )
```

time: 72.2 us -> 60.8 us (0.84)
  Pallas kernels: 67 us -> 53.2 us
  local copies, waits for them, and re-layouts: 4.35 us -> 6.64 us
    pallas_call x1, Pallas kernels: 67 us -> 53.2 us  [per_device(): pl.pallas_call(functools.partial(body, plan), out_shape=(jax.ShapeDtypeSt...]
    unnamed x15, local copies, waits for them, and re-layouts: 4.35 us -> 6.64 us
where the time goes in v2:
time: 60.8 us; the launch traced here: 60.5 us
  Pallas kernels  53.2 us (88%)
  local copies, waits for them, and re-layouts  6.64 us (11%)
  between operations  0.66 us (1%)
    pallas_call x1, Pallas kernels, per_device(): pl.pallas_call(functools.partial(body, plan), out_shape=(jax.ShapeDtypeSt...  53.2 us
    unnamed x15, local copies, waits for them, and re-layouts  6.64 us

profile of v2, /device:TPU:1, one launch (start us, length us, event | category | flops | bytes accessed | tf_op | source)
XLA Modules:
  0.0 60.5 jit_solution(3947647031011202503)
XLA Ops:
  0.6 0.0 copy-start.5
  0.6 0.0 copy-start.4
  0.7 0.7 %copy-done.5 = s32[256]{0:T(256)S(1)} copy-done((s32[256]{0:T(256)S(1)}, s32[256]{0:T(256)}, u32[]{:S(2)}) %copy-start.5) | copy-done | bytes 1048
  1.3 0.0 copy-done.4
  1.3 0.0 copy-start
  1.3 1.2 %copy-done = bf16[768,576]{0,1:T(8,128)(2,1)S(1)} copy-done((bf16[768,576]{0,1:T(8,128)(2,1)S(1)}, bf16[768,576]{0,1:T(8,128)(2,1)}, u32[]{:S(2)}) %copy-start) | copy-done | bytes 884760
  2.5 0.0 copy-start.1
  2.5 1.0 %copy-done.1 = bf16[256,768]{1,0:T(8,128)(2,1)S(1)} copy-done((bf16[256,768]{1,0:T(8,128)(2,1)S(1)}, bf16[256,768]{1,0:T(8,128)(2,1)}, u32[]{:S(2)}) %copy-start.1) | copy-done | bytes 393240
  3.5 0.0 copy-start.2
  3.5 1.0 %copy-done.2 = bf16[256,768]{1,0:T(8,128)(2,1)S(1)} copy-done((bf16[256,768]{1,0:T(8,128)(2,1)S(1)}, bf16[256,768]{1,0:T(8,128)(2,1)}, u32[]{:S(2)}) %copy-start.2) | copy-done | bytes 393240
  4.5 0.0 copy-start.3
  4.5 1.0 %copy-done.3 = bf16[192,768]{1,0:T(8,128)(2,1)S(1)} copy-done((bf16[192,768]{1,0:T(8,128)(2,1)S(1)}, bf16[192,768]{1,0:T(8,128)(2,1)}, u32[]{:S(2)}) %copy-start.3) | copy-done | bytes 294936
  5.5 53.2 %shard_map.85 = (bf16[192,256]{1,0:T(8,128)(2,1)S(1)}, f32[6,576]{1,0:T(8,128)S(1)}, f32[6,192]{1,0:T(8,128)S(1)}) custom-call(s32[2,4]{1,0:T(2,128)S(1)} %bitcast.8, s32[1,256]{1,0:T(1,128)S(1)} %bitcast.9, bf16[256,768]{1,0:T(8,128)(2,1)S(1)} %copy-done.1, bf16[576,768]{1,0:T(8,128)(2,1)S(1)} %bitcast.7, bf16[192,768]{1,0:T(8,128)(2,1)S(1)} %copy-done.3, ...), custom_call_target="tpu_custom_call" | custom-call | flops 2000000000 | bytes 4000000 | tf_op jit(solution)/shard_map/pallas_call | solution.py:401
  58.7 0.6 %copy.12 = bf16[256,192]{0,1:T(8,128)(2,1)} copy(bf16[256,192]{0,1:T(8,128)(2,1)S(1)} %bitcast.5) | data formatting | bytes 196608
  59.3 0.6 %copy.13 = f32[6,576]{1,0:T(8,128)} copy(f32[6,576]{1,0:T(8,128)S(1)} %get-tuple-element.13) | data formatting | bytes 27648
  59.9 0.6 copy.14
Async XLA Ops:
  0.6 0.7 %copy-start.5 = (s32[256]{0:T(256)S(1)}, s32[256]{0:T(256)}, u32[]{:S(2)}) copy-start(s32[256]{0:T(256)} %param.7) | copy-start | bytes 3076
  0.6 0.7 %copy-start.4 = (s32[4,2]{0,1:T(2,128)S(1)}, s32[4,2]{0,1:T(2,128)}, u32[]{:S(2)}) copy-start(s32[4,2]{0,1:T(2,128)} %param.8) | copy-start | bytes 100
  1.3 1.2 %copy-start = (bf16[768,576]{0,1:T(8,128)(2,1)S(1)}, bf16[768,576]{0,1:T(8,128)(2,1)}, u32[]{:S(2)}) copy-start(bf16[768,576]{0,1:T(8,128)(2,1)} %param.9) | copy-start | bytes 2654212
  2.5 1.0 %copy-start.1 = (bf16[256,768]{1,0:T(8,128)(2,1)S(1)}, bf16[256,768]{1,0:T(8,128)(2,1)}, u32[]{:S(2)}) copy-start(bf16[256,768]{1,0:T(8,128)(2,1)} %tokens.1) | copy-start | bytes 1179652
  3.5 1.0 %copy-start.2 = (bf16[256,768]{1,0:T(8,128)(2,1)S(1)}, bf16[256,768]{1,0:T(8,128)(2,1)}, u32[]{:S(2)}) copy-start(bf16[256,768]{1,0:T(8,128)(2,1)} %ograd.1) | copy-start | bytes 1179652
  4.5 1.0 %copy-start.3 = (bf16[192,768]{1,0:T(8,128)(2,1)S(1)}, bf16[192,768]{1,0:T(8,128)(2,1)}, u32[]{:S(2)}) copy-start(bf16[192,768]{1,0:T(8,128)(2,1)} %wout.1) | copy-start | bytes 884740

commit v3 on v2

v3 whole, which is shorter than its diff:
```python
import functools
import math

import jax
import jax.numpy as jnp
from jax import lax
from jax.experimental import pallas as pl
from jax.experimental.pallas import tpu as pltpu
from jax.sharding import PartitionSpec as P

BF = jnp.bfloat16
F32 = jnp.float32
MESH = pl.DeviceIdType.MESH

HEADS = 4
HD = 48
TOK = 256
D = 768
CORES = 2
MINE = HEADS // CORES
KV = 2 * HD * MINE
QW = HD * MINE
ALL = KV + QW
PAY = CORES * KV
ZN = 8
PAIR = 2
SPAN2 = 4
SPAN3 = 16
ROWS2 = TOK // SPAN2
ROWS3 = TOK // SPAN3
PICKED = ROWS2 + ROWS3
FAR_FIRST = (4, 3, 5, 2, 6, 1, 7)
MARK = 2.0**100
MARK_TEST = 2.0**90
LOW = -1e30
VMEM_BYTES = 58 * 1024 * 1024


def nn(a, b):
    return lax.dot_general(a, b, (((1,), (0,)), ((), ())), preferred_element_type=F32)


def nt(a, b):
    return lax.dot_general(a, b, (((1,), (1,)), ((), ())), preferred_element_type=F32)


def iota(shape, dim):
    return lax.broadcasted_iota(jnp.int32, shape, dim)


def one_hot(mask):
    return jnp.where(mask, 1.0, 0.0).astype(BF)


def thirds(x):
    high = x.astype(BF).astype(F32)
    mid = (x - high).astype(BF).astype(F32)
    return [high, mid, (x - high - mid).astype(BF).astype(F32)]


def stack_rows(rows):
    at = iota((16, rows[0].shape[1]), 0)
    out = jnp.zeros(at.shape, F32)
    for i, row in enumerate(rows):
        out = jnp.where(at == i, row, out)
    return out.astype(BF)


def halves(x):
    high = x.astype(BF)
    return [high, (x - high.astype(F32)).astype(BF)]


class Plan:
    def __init__(self, n_seq, n_head):
        self.n_head = n_head
        self.yn = 2 if n_seq >= 32 else 1
        self.xn = n_seq // (CORES * ZN * self.yn)
        self.rows_dev = D // n_seq
        self.rows_pad = -(-self.rows_dev // 8) * 8
        self.chunk = CORES * self.rows_pad
        self.rows = (n_seq // CORES) * self.chunk
        self.xrows = ZN * self.chunk
        self.lanes = self.yn * KV


def body(plan, offs_h, valid_h, tokens_h, wqkv_h, wout_h, ograd_h, gt_out, gw_out, go_out,
         offs, valid, tokens, wqkv, wout, ograd,
         p_out, s2, s3, tok_in, og_in, proj, w_loc, p_loc, kv2, kv3, g2, g3, r2, r3, own, att_t, dq_t,
         dat_t, tok_t, og_t, wn, d_out, d_in, q_out, q_in,
         xs, xr, zs, zr, ys, yr, fin, pt, pr,
         ls, es, er, a2s, a2r, a3s, a3r, b2s, b2r, b3s, b3r, ds_, dr_, cs, cr,
         xss, xrs, zss, zrs, yss, yrs):
    xn, yn, nh = plan.xn, plan.yn, plan.n_head
    factor = 1.0 / math.sqrt(HD)
    seq = lax.axis_index("seq")
    head = lax.axis_index("head")
    core = seq % CORES
    other = 1 - core
    z = (seq // CORES) % ZN
    y = (seq // (CORES * ZN)) % yn
    x = seq // (CORES * ZN * yn)

    def place(xi, yi, zi, ci):
        return (((xi * yn + yi) * ZN + zi) * CORES + ci, head)

    near_z = z % PAIR
    mate = z - near_z + 1 - near_z
    pos2 = near_z * CORES
    pos3 = z * CORES
    sibling = place(x, y, z, other)
    z_peers = {d: (z + d) % ZN for d in FAR_FIRST}
    x_peers = {d: (x + d) % xn for d in (2, 1, 3) if d < xn}
    h_peers = {d: (head + d) % nh for d in (2, 1, 3) if d < nh}
    far = (y + 1) % yn
    y_peers = [sibling]
    if yn > 1:
        y_peers += [place(x, far, z, core), place(x, far, z, other)]

    loads = []

    def load(src, dst):
        copy = pltpu.make_async_copy(src, dst, ls.at[len(loads)])
        copy.start()
        loads.append(copy)
        return copy

    def load_rows(src, dst, base, rows, pieces):
        size = rows // pieces
        return [load(src.at[at], dst.at[at]) for at in
                [pl.ds(pl.multiple_of(base + size * i, 16), size) for i in range(pieces)]]

    w_rows = MINE * 3 * HD
    need_first = [load(valid_h, valid), load(offs_h, offs)]
    need_first += load_rows(tokens_h, tokens, 0, TOK, 2)
    need_first += load_rows(wqkv_h, wqkv, 0, CORES * w_rows, 4)
    need_then = load_rows(ograd_h, ograd, 0, TOK, 2)
    need_then += load_rows(wout_h, wout, 0, CORES * QW, 1)

    barrier = pltpu.get_barrier_semaphore()
    greeted = [place(x, y, zi, c) for zi in z_peers.values() for c in (core, other)] + y_peers
    greeted += [place(xi, y, z, core) for xi in x_peers.values()]
    greeted += [(seq, to) for to in h_peers.values()]
    for who in greeted:
        pl.semaphore_signal(barrier, inc=1, device_id=who, device_id_type=MESH)

    started = []

    def send(src, dst, ssem, rsem, who):
        copy = pltpu.make_async_remote_copy(
            src_ref=src, dst_ref=dst, send_sem=ssem, recv_sem=rsem,
            device_id=who, device_id_type=MESH)
        copy.start()
        started.append(copy)
        return copy

    def qkv_of(c):
        base = c * w_rows
        rows = [wqkv[pl.ds(pl.multiple_of(base + 3 * HD * h + HD, 16), 2 * HD), :]
                for h in range(MINE)]
        rows += [wqkv[pl.ds(pl.multiple_of(base + 3 * HD * h, 16), HD), :]
                 for h in range(MINE)]
        return jnp.concatenate(rows, axis=0)

    def out_of(c):
        return wout[pl.ds(pl.multiple_of(c * QW, 16), QW), :]

    eye = iota((TOK, TOK), 0) == iota((TOK, TOK), 1)
    eye_b = one_hot(eye)
    lane = iota((TOK, ALL), 1)
    can_mark = (lane % (2 * HD) == 0) & (lane < KV)
    for copy in need_first:
        copy.wait()
    alive = jnp.sum(jnp.where(eye, valid[...].astype(F32), 0.0), axis=1, keepdims=True)
    marked = can_mark & (alive == 0.0)
    w_mine, w_other = qkv_of(core), qkv_of(other)
    proj[0, :, :ALL] = jnp.where(marked, MARK, nt(tokens[...], w_mine)).astype(BF)
    p_out[:, :ALL] = jnp.where(marked, MARK, nt(tokens[...], w_other)).astype(BF)

    def pick_of(g):
        rows = iota((PICKED, TOK), 0)
        want = jnp.where(rows < ROWS2, rows * SPAN2 + offs[0, g],
                         (rows - ROWS2) * SPAN3 + offs[1, g])
        return one_hot(iota((PICKED, TOK), 1) == want)

    picks = [pick_of(core * MINE + h) for h in range(MINE)]
    for h in range(MINE):
        cols = slice(2 * HD * h, 2 * HD * (h + 1))
        chosen = nn(picks[h], proj[0, :, cols]).astype(BF)
        kv2[pos2, :, cols] = chosen[:ROWS2]
        kv3[pos3, :, cols] = chosen[ROWS2:]
        chosen = nn(pick_of(other * MINE + h), p_out[:, cols]).astype(BF)
        s2[:, cols] = chosen[:ROWS2]
        s3[:, cols] = chosen[ROWS2:]

    pl.semaphore_wait(barrier, len(greeted))
    a_copies = []

    def spread_out(d, zi, c, same):
        if d in (0, 4):
            to = mate if d else z
            a_copies.append(send(kv2.at[pos2] if same else s2, kv2.at[pos2 + 1 - same],
                                 a2s.at[d // 4, same], a2r.at[d // 4, same], place(x, y, to, c)))
        a_copies.append(send(kv3.at[pos3] if same else s3, kv3.at[pos3 + 1 - same],
                             a3s.at[d, same], a3r.at[d, same], place(x, y, zi, c)))

    for d, zi in z_peers.items():
        spread_out(d, zi, core, 1)
        spread_out(d, zi, other, 0)
    spread_out(0, z, other, 0)

    for copy in need_then:
        copy.wait()
    p_out[:, ALL:] = nt(ograd[...], out_of(other)).astype(BF)
    swap = send(p_out, proj.at[1], es.at[0], er.at[0], sibling)
    tok_swap = send(tokens, tok_in, es.at[1], er.at[1], sibling)
    og_swap = send(ograd, og_in, es.at[2], er.at[2], sibling)

    phase2 = [offs[0, core * MINE + h] for h in range(MINE)]
    phase3 = [offs[1, core * MINE + h] for h in range(MINE)]
    proj[0, :, ALL:] = nt(ograd[...], out_of(core)).astype(BF)
    dat_t[:, :TOK] = nt(out_of(core), ograd[...]).astype(BF)
    swap.wait_recv()
    dat_t[:, TOK:] = nt(eye_b[:QW, :QW], proj[1, :, ALL:]).astype(BF)
    eye_kv = one_hot(iota((KV, KV), 0) == iota((KV, KV), 1))
    local_t = [nt(eye_kv, proj[b, :, :KV]).astype(BF) for b in range(2)]
    spots = []
    for h in range(MINE):
        zero2, zero3 = jnp.zeros((ROWS2, TOK), BF), jnp.zeros((ROWS3, TOK), BF)
        one2, one3 = picks[h][:ROWS2], picks[h][ROWS2:]
        spots.append([
            jnp.concatenate([jnp.concatenate([one, zero], axis=1),
                             jnp.concatenate([zero, one], axis=1)], axis=0)
            for one, zero in ((one2, zero2), (one3, zero3))])

    def columns(h):
        return (slice(2 * HD * h, 2 * HD * h + HD), slice(2 * HD * h + HD, 2 * HD * (h + 1)),
                slice(KV + HD * h, KV + HD * (h + 1)), slice(ALL + HD * h, ALL + HD * (h + 1)))

    def soft(k, q):
        keep = k[:, 0:1].astype(F32) < MARK_TEST
        s = jnp.where(keep, nt(k, q) * factor, LOW)
        peak = jnp.max(s, axis=0, keepdims=True)
        w = jnp.exp(s - peak)
        return peak, w, jnp.sum(w, axis=0, keepdims=True)

    local = []
    few = []
    for h in range(MINE):
        kc, vc, qc, dc = columns(h)
        parts = []
        for b in range(2):
            peak, w, den = soft(proj[b, :, kc], proj[b, :, qc])
            w_loc[h, b] = w
            p_loc[h, b] = nt(proj[b, :, vc], proj[b, :, dc])
            parts.append((peak, den, nn(local_t[b][vc, :], w.astype(BF))))
        local.append([jnp.concatenate([parts[0][i], parts[1][i]], axis=1) for i in range(3)])
        chosen = [[nn(picks[h], proj[b, :, c]).astype(BF) for b in range(2)] for c in (qc, dc)]
        few.append([[jnp.concatenate([pair[0][at], pair[1][at]], axis=0) for pair in chosen]
                    for at in (slice(0, ROWS2), slice(ROWS2, PICKED))])

    half = plan.rows // 2
    rr = iota((half, 1), 0)
    inner = rr % plan.chunk
    j = inner % plan.rows_pad
    source = jnp.where(
        j < plan.rows_dev,
        ((rr // plan.chunk) * CORES + inner // plan.rows_pad) * plan.rows_dev + j, -1)
    place_rows = one_hot(iota((half, D // 2), 1) == source)

    def place_block(to, block, b):
        for part in range(2):
            cols = slice(part * D // 2, (part + 1) * D // 2)
            to[part * half:(part + 1) * half, b * TOK:(b + 1) * TOK] = nt(
                place_rows, block[:, cols]).astype(BF)

    place_block(tok_t, tokens, 0)
    place_block(og_t, ograd, 0)
    eye_d = one_hot(iota((D, D), 0) == iota((D, D), 1))
    wn[0] = nt(eye_d, w_mine).astype(BF)
    wn[1] = nt(eye_d, w_other).astype(BF)

    for copy in a_copies:
        copy.wait_recv()

    lane = iota((1, 2 * TOK), 1)
    rows_far = [kv2[...].reshape(TOK, KV), kv3[...].reshape(TOK, KV)]
    cols_far = [nt(eye_kv, r).astype(BF) for r in rows_far]
    scale_loc, delta_loc, dq_far = [], [], []
    for h in range(MINE):
        kc, vc, _, _ = columns(h)
        inside = [lane % SPAN2 == phase2[h], lane % SPAN3 == phase3[h]]
        peaks, dens, nums, far_w = [local[h][0]], [local[h][1]], [local[h][2]], []
        for level in range(2):
            peak, w, den = soft(rows_far[level][:, kc], few[h][level][0])
            num = nn(cols_far[level][vc, :], w.astype(BF))
            got = nn(jnp.concatenate([stack_rows(thirds(peak) + thirds(den))] + halves(num), axis=0),
                     spots[h][level])
            peaks.append(jnp.where(inside[level], got[0:1] + got[1:2] + got[2:3], LOW))
            dens.append(got[3:4] + got[4:5] + got[5:6])
            nums.append(got[16:16 + HD] + got[16 + HD:16 + 2 * HD])
            far_w.append(w)
        top = jnp.maximum(jnp.maximum(peaks[0], peaks[1]), peaks[2])
        scales = [jnp.exp(peak - top) for peak in peaks]
        inv = 1.0 / sum(scale * den for scale, den in zip(scales, dens))
        att = (sum(scale * num for scale, num in zip(scales, nums)) * inv).astype(BF)
        hr = slice(HD * h, HD * (h + 1))
        att_t[hr, :] = att
        delta = jnp.sum(dat_t[hr, :].astype(F32) * att.astype(F32), axis=0, keepdims=True)
        scale_loc.append(scales[0] * inv)
        delta_loc.append(delta)
        wanted = stack_rows(thirds(scales[1] * inv) + thirds(scales[2] * inv) + thirds(delta))
        dq = None
        for level, (to, n) in enumerate(((g2, PAIR), (g3, ZN))):
            got = nt(wanted, spots[h][level])
            i = 3 * level
            scale = got[i:i + 1] + got[i + 1:i + 2] + got[i + 2:i + 3]
            delta_few = got[6:7] + got[7:8] + got[8:9]
            normed = far_w[level] * scale
            q, d = few[h][level]
            grad = (normed * (nt(rows_far[level][:, vc], d) - delta_few)).astype(BF)
            dk = (nn(grad, q) * factor).astype(BF).reshape(n, CORES, -1, HD)
            dv = nn(normed.astype(BF), d).astype(BF).reshape(n, CORES, -1, HD)
            for part in range(CORES):
                put = part * KV
                to[:, :, put + kc.start:put + kc.stop] = dk[:, part]
                to[:, :, put + vc.start:put + vc.stop] = dv[:, part]
            back = nn(jnp.concatenate(halves(nn(cols_far[level][kc, :], grad)), axis=0),
                      spots[h][level])
            part = back[:HD] + back[HD:]
            dq = part if dq is None else dq + part
        dq_far.append(dq)

    b_copies = []
    for d, zi in z_peers.items():
        b_copies.append(send(g3.at[zi], r3.at[z], b3s.at[d], b3r.at[d], place(x, y, zi, core)))
        if d == 4:
            b_copies.append(send(g2.at[1 - near_z], r2.at[near_z], b2s, b2r,
                                 place(x, y, mate, core)))
    r2[near_z] = g2[near_z]
    r3[z] = g3[z]

    for h in range(MINE):
        kc, vc, qc, dc = columns(h)
        for b in range(2):
            at = slice(b * TOK, (b + 1) * TOK)
            normed = w_loc[h, b] * scale_loc[h][:, at]
            grad = (normed * (p_loc[h, b] - delta_loc[h][:, at])).astype(BF)
            own[b, :, kc] = nn(grad, proj[b, :, qc]) * factor
            own[b, :, vc] = nn(normed.astype(BF), proj[b, :, dc])
            dq = nn(local_t[b][kc, :], grad) + dq_far[h][:, at]
            dq_t[HD * h:HD * (h + 1), at] = (dq * factor).astype(BF)

    def pack(i, col, block):
        width = block.shape[1]
        block = block.astype(BF).reshape(xn, yn, plan.xrows, width)
        for yi in range(yn):
            xs[i, :, :, yi * KV + col:yi * KV + col + width] = block[:, yi]

    def parts_of(i):
        count = 2 if i else 1
        size = plan.xrows // count
        return [(k, pl.ds(k * size, size)) for k in range(count)]

    def start_x(i):
        return [[send(xs.at[i, xi, at], xr.at[i, d, at], xss.at[i, k, d], xrs.at[i, k, d],
                      place(xi, y, z, core)) for d, xi in x_peers.items()]
                for k, at in parts_of(i)]

    def start_z(i, copies):
        parts = parts_of(i)
        deep = ZN // len(parts)
        flying = {}
        for (k, at), some in zip(parts, copies):
            total = xs[i, x, at].astype(F32)
            for d, copy in zip(x_peers, some):
                copy.wait_recv()
                total = total + xr[i, d, at].astype(F32)
            zs[i, k * deep:(k + 1) * deep] = total.astype(BF).reshape(
                deep, plan.chunk, plan.lanes)
            for d, zi in z_peers.items():
                copy = pltpu.make_async_remote_copy(
                    src_ref=zs.at[i, zi], dst_ref=zr.at[i, d], send_sem=zss.at[i, d],
                    recv_sem=zrs.at[i, d], device_id=place(x, y, zi, core),
                    device_id_type=MESH)
                flying[d] = copy
                if len(parts) == 1:
                    copy.start()
                else:
                    pl.when(zi // deep == k)(copy.start)
        started.extend(flying.values())
        return flying

    def start_y(i, copies):
        total = zs[i, z].astype(F32)
        for d, copy in copies.items():
            copy.wait_recv()
            total = total + zr[i, d].astype(F32)
        ys[i] = total.astype(BF)
        return [send(ys.at[i], yr.at[d, i], yss.at[d, i], yrs.at[d, i], who)
                for d, who in enumerate(y_peers)]

    dq = [nt(eye_b, dq_t[:, b * TOK:(b + 1) * TOK]).astype(BF) for b in range(2)]
    q_out[...] = dq[1]
    q_swap = send(q_out, q_in, ds_.at[0], dr_.at[0], sibling)
    og_swap.wait_recv()
    place_block(og_t, og_in, 1)
    pack(0, 0, nt(og_t[...], att_t[...]))
    tok_swap.wait_recv()
    place_block(tok_t, tok_in, 1)
    pack(0, QW, nt(tok_t[...], dq_t[...]))
    x_first = start_x(0)
    spreads = []
    for h in range(MINE):
        row, col = iota((TOK, TOK), 0), iota((TOK, TOK), 1)
        spreads.append(one_hot(row == jnp.where(
            col < PAIR * ROWS2, (col % ROWS2) * SPAN2 + phase2[h],
            (col % ROWS3) * SPAN3 + phase3[h])))
    for copy in b_copies:
        copy.wait_recv()
    back = jnp.concatenate([r2[...].reshape(PAIR * ROWS2, PAY),
                            r3[...].reshape(ZN * ROWS3, PAY)], axis=0)

    def finish(b):
        parts = []
        for h in range(MINE):
            cols = slice(2 * HD * h, 2 * HD * (h + 1))
            got = slice(b * KV + 2 * HD * h, b * KV + 2 * HD * (h + 1))
            parts.append(own[b, :, cols] + nn(spreads[h], back[:, got]))
        return jnp.concatenate(parts, axis=1).astype(BF)

    theirs = finish(1)
    d_out[...] = theirs
    swap = send(d_out, d_in, ds_.at[1], dr_.at[1], sibling)
    mine = finish(0)
    pack(1, 0, nn(tok_t[...], jnp.concatenate([mine, theirs], axis=0)))
    x_second = start_x(1)

    shares = nt(wn[0], jnp.concatenate([mine, dq[0]], axis=1))
    q_swap.wait_recv()
    swap.wait_recv()
    shares = shares + nt(wn[1], jnp.concatenate([d_in[...], q_in[...]], axis=1))
    pt[...] = shares.astype(BF).reshape(pt.shape)
    c_copies = []
    for d, to in h_peers.items():
        c_copies.append(send(pt.at[to], pr.at[d], cs.at[d], cr.at[d], (seq, to)))

    z_first = start_z(0, x_first)
    z_second = start_z(1, x_second)
    y_first = start_y(0, z_first)
    y_second = start_y(1, z_second)

    total = pt[head].astype(F32)
    for d, copy in zip(h_peers, c_copies):
        copy.wait_recv()
        total = total + pr[d].astype(F32)
    gt_out[...] = total.astype(BF)

    for i, copies in enumerate((y_first, y_second)):
        for copy in copies:
            copy.wait_recv()
        mine = ys[i].astype(F32)
        theirs = yr[0, i].astype(F32)
        if yn > 1:
            mine = mine + yr[1, i].astype(F32)
            theirs = theirs + yr[2, i].astype(F32)
            mine = jnp.where(y == 0, mine[:, :KV], mine[:, KV:])
            theirs = jnp.where(y == 0, theirs[:, :KV], theirs[:, KV:])
        fin[core, :, i * KV:(i + 1) * KV] = mine
        fin[other, :, i * KV:(i + 1) * KV] = theirs
    rows = pl.ds(pl.multiple_of(core * plan.rows_pad, 8), plan.rows_pad)
    done = [fin[c, rows, :][:plan.rows_dev] for c in range(CORES)]
    go_out[...] = jnp.concatenate([f[:, :QW] for f in done], axis=1)
    gw_out[...] = jnp.concatenate(
        [piece for f in done for h in range(MINE)
         for piece in (f[:, QW + HD * h:QW + HD * (h + 1)],
                       f[:, KV + 2 * HD * h:KV + 2 * HD * (h + 1)])], axis=1)
    for copy in started:
        copy.wait_send()


def write_out(gt, gw, go, gt_out, gw_out, go_out, sems):
    copies = [pltpu.make_async_copy(a, b, sems.at[i]) for i, (a, b) in enumerate(
        ((gt, gt_out), (gw, gw_out), (go, go_out)))]
    for copy in copies:
        copy.start()
    for copy in copies:
        copy.wait()


def per_device(plan, tokens, valid, offsets, qkv_weight, out_weight, out_grad):
    vm = pl.BlockSpec(memory_space=pltpu.VMEM)
    hbm = pl.BlockSpec(memory_space=pltpu.HBM)
    dma = pltpu.SemaphoreType.DMA
    xn, rows, lanes = plan.xn, plan.rows, plan.lanes
    near, wide = pltpu.VMEM((PAIR, ROWS2, PAY), BF), pltpu.VMEM((ZN, ROWS3, PAY), BF)
    square = pltpu.VMEM((MINE, 2, TOK, TOK), F32)
    scratch = [
        pltpu.SMEM((2, HEADS), jnp.int32),
        pltpu.VMEM((1, TOK), jnp.int32),
        pltpu.VMEM((TOK, D), BF),
        pltpu.VMEM((HEADS * 3 * HD, D), BF),
        pltpu.VMEM((HEADS * HD, D), BF),
        pltpu.VMEM((TOK, D), BF),
        pltpu.VMEM((TOK, ALL + QW), BF),
        pltpu.VMEM((ROWS2, KV), BF),
        pltpu.VMEM((ROWS3, KV), BF),
        pltpu.VMEM((TOK, D), BF),
        pltpu.VMEM((TOK, D), BF),
        pltpu.VMEM((2, TOK, ALL + QW), BF),
        square, square,
        pltpu.VMEM((PAIR * CORES, ROWS2, KV), BF),
        pltpu.VMEM((ZN * CORES, ROWS3, KV), BF),
        near, wide, near, wide,
        pltpu.VMEM((2, TOK, KV), F32),
        pltpu.VMEM((QW, 2 * TOK), BF),
        pltpu.VMEM((QW, 2 * TOK), BF),
        pltpu.VMEM((QW, 2 * TOK), BF),
        pltpu.VMEM((rows, 2 * TOK), BF),
        pltpu.VMEM((rows, 2 * TOK), BF),
        pltpu.VMEM((2, D, ALL), BF),
        pltpu.VMEM((TOK, KV), BF),
        pltpu.VMEM((TOK, KV), BF),
        pltpu.VMEM((TOK, QW), BF),
        pltpu.VMEM((TOK, QW), BF),
        pltpu.VMEM((2, xn, plan.xrows, lanes), BF),
        pltpu.VMEM((2, xn, plan.xrows, lanes), BF),
        pltpu.VMEM((2, ZN, plan.chunk, lanes), BF),
        pltpu.VMEM((2, ZN, plan.chunk, lanes), BF),
        pltpu.VMEM((2, plan.chunk, lanes), BF),
        pltpu.VMEM((3, 2, plan.chunk, lanes), BF),
        pltpu.VMEM((2, plan.chunk, 2 * KV), F32),
        pltpu.VMEM((4, D // 4, TOK), BF),
        pltpu.VMEM((4, D // 4, TOK), BF),
        dma((16,)), dma((3,)), dma((3,)),
        dma((2, 2)), dma((2, 2)), dma((ZN, 2)), dma((ZN, 2)),
        dma, dma, dma((ZN,)), dma((ZN,)), dma((2,)), dma((2,)), dma((4,)), dma((4,)),
        dma((2, 2, 4)), dma((2, 2, 4)), dma((2, ZN)), dma((2, ZN)), dma((3, 2)), dma((3, 2)),
    ]
    gt, gw, go = pl.pallas_call(
        functools.partial(body, plan),
        out_shape=(
            jax.ShapeDtypeStruct((D // 4, TOK), BF),
            jax.ShapeDtypeStruct((plan.rows_dev, HEADS * 3 * HD), F32),
            jax.ShapeDtypeStruct((plan.rows_dev, HEADS * HD), F32),
        ),
        in_specs=[hbm] * 6,
        out_specs=(vm, vm, vm),
        scratch_shapes=scratch,
        compiler_params=pltpu.CompilerParams(
            collective_id=0, has_side_effects=True, vmem_limit_bytes=VMEM_BYTES),
        cost_estimate=pl.CostEstimate(flops=2_000_000_000, bytes_accessed=4_000_000,
                                      transcendentals=800_000),
    )(offsets.T, valid.reshape(1, TOK), tokens, qkv_weight.T, out_weight, out_grad)
    hold = pl.pallas_call(
        write_out,
        out_shape=tuple(jax.ShapeDtypeStruct(a.shape, a.dtype) for a in (gt, gw, go)),
        in_specs=[hbm] * 3,
        out_specs=(hbm, hbm, hbm),
        scratch_shapes=[dma((3,))],
        compiler_params=pltpu.CompilerParams(vmem_limit_bytes=VMEM_BYTES),
    )(gt, gw, go)
    return hold[0].T, hold[1], hold[2].T


def solution(mesh):
    plan = Plan(mesh.shape["seq"], mesh.shape["head"])
    return jax.shard_map(
        functools.partial(per_device, plan),
        mesh=mesh,
        in_specs=(
            P("seq", None),
            P("seq"),
            P("head", None),
            P(None, "head"),
            P("head", None),
            P("seq", None),
        ),
        out_specs=(P("seq", "head"), P("seq", "head"), P("head", "seq")),
        check_vma=False,
    )
```

time: 60.8 us -> 53.3 us (0.88)
  local copies, waits for them, and re-layouts: 6.64 us -> 0 us
  Pallas kernels: 53.2 us -> 52.5 us
    unnamed x15 -> x0, local copies, waits for them, and re-layouts: 6.64 us -> none
    pallas_call x1, Pallas kernels: 53.2 us -> 47.6 us  [per_device(): pl.pallas_call(functools.partial(body, plan), out_shape=(jax.ShapeDtypeSt...]
    pallas_call x0 -> x1, Pallas kernels: none -> 4.98 us  [per_device(): pl.pallas_call(write_out, out_shape=tuple((jax.ShapeDtypeStruct(a.shape,...]
where the time goes in v3:
time: 53.3 us; the launch traced here: 53.2 us
  Pallas kernels  52.5 us (98%)
  between operations  0.64 us (1%)
    pallas_call x1, Pallas kernels, per_device(): pl.pallas_call(functools.partial(body, plan), out_shape=(jax.ShapeDtypeSt...  47.6 us
    pallas_call x1, Pallas kernels, per_device(): pl.pallas_call(write_out, out_shape=tuple((jax.ShapeDtypeStruct(a.shape,...  4.98 us

profile of v3, /device:TPU:1, one launch (start us, length us, event | category | flops | bytes accessed | tf_op | source)
XLA Modules:
  0.0 53.2 jit_solution(1366998869016914262)
XLA Ops:
  0.6 47.6 %shard_map.85 = (bf16[192,256]{1,0:T(8,128)(2,1)}, f32[6,576]{1,0:T(8,128)}, f32[6,192]{1,0:T(8,128)}) custom-call(s32[2,4]{1,0:T(2,128)} %bitcast.8, s32[1,256]{1,0:T(1,128)} %bitcast.9, bf16[256,768]{1,0:T(8,128)(2,1)} %tokens_h.1, bf16[576,768]{1,0:T(8,128)(2,1)} %bitcast.5, bf16[192,768]{1,0:T(8,128)(2,1)} %wout_h.1, bf16[256,768]{1,0:T(8,128)(2,1)} %ograd_h.1), custom_call_target="tpu_custom_call" | custom-call | flops 2000000000 | bytes 4000000 | tf_op jit(solution)/shard_map/pallas_call | solution.py:540
  48.2 5.0 %shard_map.86 = (bf16[192,256]{1,0:T(8,128)(2,1)}, f32[6,576]{1,0:T(8,128)}, f32[6,192]{1,0:T(8,128)}) custom-call(bf16[192,256]{1,0:T(8,128)(2,1)} %get-tuple-element.9.gt, f32[6,576]{1,0:T(8,128)} %get-tuple-element.10.gw, f32[6,192]{1,0:T(8,128)} %get-tuple-element.11.go), custom_call_target="tpu_custom_call" | custom-call | tf_op jit(solution)/shard_map/pallas_call | solution.py:555

commit v4 on v3

--- a/solution.py
+++ b/solution.py
@@ -77,10 +77,9 @@
         self.yn = 2 if n_seq >= 32 else 1
         self.xn = n_seq // (CORES * ZN * self.yn)
         self.rows_dev = D // n_seq
-        self.rows_pad = -(-self.rows_dev // 8) * 8
-        self.chunk = CORES * self.rows_pad
-        self.rows = (n_seq // CORES) * self.chunk
-        self.xrows = ZN * self.chunk
+        self.rows_chip = CORES * self.rows_dev
+        self.chunk = -(-self.rows_chip // 16) * 16
+        self.xrows = ZN * self.rows_chip
         self.lanes = self.yn * KV
 
 
@@ -88,7 +87,7 @@
          offs, valid, tokens, wqkv, wout, ograd,
          p_out, s2, s3, tok_in, og_in, proj, w_loc, p_loc, kv2, kv3, g2, g3, r2, r3, own, att_t, dq_t,
          dat_t, tok_t, og_t, wn, d_out, d_in, q_out, q_in,
-         xs, xr, zs, zr, ys, yr, fin, pt, pr,
+         xs, xr, zs, zr, ys, yr, pt, pr, pv,
          ls, es, er, a2s, a2r, a3s, a3r, b2s, b2r, b3s, b3r, ds_, dr_, cs, cr,
          xss, xrs, zss, zrs, yss, yrs):
     xn, yn, nh = plan.xn, plan.yn, plan.n_head
@@ -111,7 +110,7 @@
     sibling = place(x, y, z, other)
     z_peers = {d: (z + d) % ZN for d in FAR_FIRST}
     x_peers = {d: (x + d) % xn for d in (2, 1, 3) if d < xn}
-    h_peers = {d: (head + d) % nh for d in (2, 1, 3) if d < nh}
+    h_peers = {d: (head + d) % nh for d in (1, 3) if d < nh}
     far = (y + 1) % yn
     y_peers = [sibling]
     if yn > 1:
@@ -196,18 +195,18 @@
     pl.semaphore_wait(barrier, len(greeted))
     a_copies = []
 
-    def spread_out(d, zi, c, same):
-        if d in (0, 4):
-            to = mate if d else z
-            a_copies.append(send(kv2.at[pos2] if same else s2, kv2.at[pos2 + 1 - same],
-                                 a2s.at[d // 4, same], a2r.at[d // 4, same], place(x, y, to, c)))
-        a_copies.append(send(kv3.at[pos3] if same else s3, kv3.at[pos3 + 1 - same],
-                             a3s.at[d, same], a3r.at[d, same], place(x, y, zi, c)))
+    def give(source, other_source, to, sems, at, slot, zi, c):
+        same = 0 if c is other else 1
+        a_copies.append(send(source if same else other_source, to.at[slot + 1 - same],
+                             sems[0].at[at, same], sems[1].at[at, same], place(x, y, zi, c)))
 
     for d, zi in z_peers.items():
-        spread_out(d, zi, core, 1)
-        spread_out(d, zi, other, 0)
-    spread_out(0, z, other, 0)
+        for c in (core, other):
+            give(kv3.at[pos3], s3, kv3, (a3s, a3r), d, pos3, zi, c)
+    for c in (core, other):
+        give(kv2.at[pos2], s2, kv2, (a2s, a2r), 1, pos2, mate, c)
+    give(kv3.at[pos3], s3, kv3, (a3s, a3r), 0, pos3, z, other)
+    give(kv2.at[pos2], s2, kv2, (a2s, a2r), 0, pos2, z, other)
 
     for copy in need_then:
         copy.wait()
@@ -259,23 +258,16 @@
         few.append([[jnp.concatenate([pair[0][at], pair[1][at]], axis=0) for pair in chosen]
                     for at in (slice(0, ROWS2), slice(ROWS2, PICKED))])
 
-    half = plan.rows // 2
-    rr = iota((half, 1), 0)
-    inner = rr % plan.chunk
-    j = inner % plan.rows_pad
-    source = jnp.where(
-        j < plan.rows_dev,
-        ((rr // plan.chunk) * CORES + inner // plan.rows_pad) * plan.rows_dev + j, -1)
-    place_rows = one_hot(iota((half, D // 2), 1) == source)
-
-    def place_block(to, block, b):
+    half = D // 2
+    eye_half = one_hot(iota((half, half), 0) == iota((half, half), 1))
+
+    def turn(to, block, b):
         for part in range(2):
-            cols = slice(part * D // 2, (part + 1) * D // 2)
-            to[part * half:(part + 1) * half, b * TOK:(b + 1) * TOK] = nt(
-                place_rows, block[:, cols]).astype(BF)
-
-    place_block(tok_t, tokens, 0)
-    place_block(og_t, ograd, 0)
+            at = slice(part * half, (part + 1) * half)
+            to[at, b * TOK:(b + 1) * TOK] = nt(eye_half, block[:, at]).astype(BF)
+
+    turn(tok_t, tokens, 0)
+    turn(og_t, ograd, 0)
     eye_d = one_hot(iota((D, D), 0) == iota((D, D), 1))
     wn[0] = nt(eye_d, w_mine).astype(BF)
     wn[1] = nt(eye_d, w_other).astype(BF)
@@ -334,9 +326,7 @@
     b_copies = []
     for d, zi in z_peers.items():
         b_copies.append(send(g3.at[zi], r3.at[z], b3s.at[d], b3r.at[d], place(x, y, zi, core)))
-        if d == 4:
-            b_copies.append(send(g2.at[1 - near_z], r2.at[near_z], b2s, b2r,
-                                 place(x, y, mate, core)))
+    b_copies.append(send(g2.at[1 - near_z], r2.at[near_z], b2s, b2r, place(x, y, mate, core)))
     r2[near_z] = g2[near_z]
     r3[z] = g3[z]
 
@@ -367,7 +357,7 @@
                       place(xi, y, z, core)) for d, xi in x_peers.items()]
                 for k, at in parts_of(i)]
 
-    def start_z(i, copies):
+    def start_z(i, copies, between=None):
         parts = parts_of(i)
         deep = ZN // len(parts)
         flying = {}
@@ -376,8 +366,12 @@
             for d, copy in zip(x_peers, some):
                 copy.wait_recv()
                 total = total + xr[i, d, at].astype(F32)
-            zs[i, k * deep:(k + 1) * deep] = total.astype(BF).reshape(
-                deep, plan.chunk, plan.lanes)
+            for j in range(deep):
+                rows = total[j * plan.rows_chip:(j + 1) * plan.rows_chip]
+                if plan.chunk > plan.rows_chip:
+                    rest = jnp.zeros((plan.chunk - plan.rows_chip, plan.lanes), F32)
+                    rows = jnp.concatenate([rows, rest], axis=0)
+                zs[i, k * deep + j] = rows.astype(BF)
             for d, zi in z_peers.items():
                 copy = pltpu.make_async_remote_copy(
                     src_ref=zs.at[i, zi], dst_ref=zr.at[i, d], send_sem=zss.at[i, d],
@@ -388,6 +382,8 @@
                     copy.start()
                 else:
                     pl.when(zi // deep == k)(copy.start)
+            if between is not None and k == 0:
+                between()
         started.extend(flying.values())
         return flying
 
@@ -404,10 +400,10 @@
     q_out[...] = dq[1]
     q_swap = send(q_out, q_in, ds_.at[0], dr_.at[0], sibling)
     og_swap.wait_recv()
-    place_block(og_t, og_in, 1)
+    turn(og_t, og_in, 1)
     pack(0, 0, nt(og_t[...], att_t[...]))
     tok_swap.wait_recv()
-    place_block(tok_t, tok_in, 1)
+    turn(tok_t, tok_in, 1)
     pack(0, QW, nt(tok_t[...], dq_t[...]))
     x_first = start_x(0)
     spreads = []
@@ -441,58 +437,78 @@
     swap.wait_recv()
     shares = shares + nt(wn[1], jnp.concatenate([d_in[...], q_in[...]], axis=1))
     pt[...] = shares.astype(BF).reshape(pt.shape)
-    c_copies = []
-    for d, to in h_peers.items():
-        c_copies.append(send(pt.at[to], pr.at[d], cs.at[d], cr.at[d], (seq, to)))
+    c_far, c_near = [], []
+    cut = D // 8
+    if nh > 1:
+        ring = [((head + 1) % nh, 0), ((head + nh - 1) % nh, 1)]
+        over = (head + 2) % nh
+
+        def hand(src, slot, way, to):
+            return send(src, pr.at[slot, way], cs.at[slot, way], cr.at[slot, way], (seq, to))
+
+        for to, way in ring:
+            c_far.append(hand(pt.at[over, pl.ds(way * cut, cut)], 0, way, to))
+        for to, way in ring:
+            c_near.append(hand(pt.at[to, pl.ds((1 - way) * cut, cut)], 1, way, to))
+
+    def pass_on():
+        for copy, (to, way) in zip(c_far, ring if nh > 1 else []):
+            copy.wait_recv()
+            both = pt[to, way * cut:(way + 1) * cut].astype(F32) + pr[0, way].astype(F32)
+            pv[way] = both.astype(BF)
+            c_near.append(hand(pv.at[way], 2, way, to))
 
     z_first = start_z(0, x_first)
-    z_second = start_z(1, x_second)
+    z_second = start_z(1, x_second, pass_on)
     y_first = start_y(0, z_first)
     y_second = start_y(1, z_second)
 
     total = pt[head].astype(F32)
-    for d, copy in zip(h_peers, c_copies):
+    for copy in c_near:
         copy.wait_recv()
-        total = total + pr[d].astype(F32)
+    if nh > 1:
+        low = total[:cut] + pr[2, 0].astype(F32) + pr[1, 1].astype(F32)
+        high = total[cut:] + pr[2, 1].astype(F32) + pr[1, 0].astype(F32)
+        total = jnp.concatenate([low, high], axis=0)
     gt_out[...] = total.astype(BF)
 
+    sums = []
     for i, copies in enumerate((y_first, y_second)):
         for copy in copies:
             copy.wait_recv()
-        mine = ys[i].astype(F32)
-        theirs = yr[0, i].astype(F32)
+        own_part = ys[i].astype(F32)
+        far_part = yr[0, i].astype(F32)
         if yn > 1:
-            mine = mine + yr[1, i].astype(F32)
-            theirs = theirs + yr[2, i].astype(F32)
-            mine = jnp.where(y == 0, mine[:, :KV], mine[:, KV:])
-            theirs = jnp.where(y == 0, theirs[:, :KV], theirs[:, KV:])
-        fin[core, :, i * KV:(i + 1) * KV] = mine
-        fin[other, :, i * KV:(i + 1) * KV] = theirs
-    rows = pl.ds(pl.multiple_of(core * plan.rows_pad, 8), plan.rows_pad)
-    done = [fin[c, rows, :][:plan.rows_dev] for c in range(CORES)]
-    go_out[...] = jnp.concatenate([f[:, :QW] for f in done], axis=1)
+            own_part = own_part + yr[1, i].astype(F32)
+            far_part = far_part + yr[2, i].astype(F32)
+            own_part = jnp.where(y == 0, own_part[:, :KV], own_part[:, KV:])
+            far_part = jnp.where(y == 0, far_part[:, :KV], far_part[:, KV:])
+        n = plan.rows_dev
+        own_part, far_part = [jnp.where(core == 0, a[:n], a[n:2 * n])
+                              for a in (own_part, far_part)]
+        sums.append([jnp.where(core == 0, own_part, far_part),
+                     jnp.where(core == 0, far_part, own_part)])
+    early, late = sums
+    go_out[...] = jnp.concatenate([early[c][:, :QW] for c in range(CORES)], axis=1)
     gw_out[...] = jnp.concatenate(
-        [piece for f in done for h in range(MINE)
-         for piece in (f[:, QW + HD * h:QW + HD * (h + 1)],
-                       f[:, KV + 2 * HD * h:KV + 2 * HD * (h + 1)])], axis=1)
+        [piece for c in range(CORES) for h in range(MINE)
+         for piece in (early[c][:, QW + HD * h:QW + HD * (h + 1)],
+                       late[c][:, 2 * HD * h:2 * HD * (h + 1)])], axis=1)
     for copy in started:
         copy.wait_send()
 
 
-def write_out(gt, gw, go, gt_out, gw_out, go_out, sems):
-    copies = [pltpu.make_async_copy(a, b, sems.at[i]) for i, (a, b) in enumerate(
-        ((gt, gt_out), (gw, gw_out), (go, go_out)))]
-    for copy in copies:
-        copy.start()
-    for copy in copies:
-        copy.wait()
+def write_out(gt, gw, go, gt_out, gw_out, go_out):
+    gt_out[...] = gt[...]
+    gw_out[...] = gw[...]
+    go_out[...] = go[...]
 
 
 def per_device(plan, tokens, valid, offsets, qkv_weight, out_weight, out_grad):
     vm = pl.BlockSpec(memory_space=pltpu.VMEM)
     hbm = pl.BlockSpec(memory_space=pltpu.HBM)
     dma = pltpu.SemaphoreType.DMA
-    xn, rows, lanes = plan.xn, plan.rows, plan.lanes
+    xn, lanes = plan.xn, plan.lanes
     near, wide = pltpu.VMEM((PAIR, ROWS2, PAY), BF), pltpu.VMEM((ZN, ROWS3, PAY), BF)
     square = pltpu.VMEM((MINE, 2, TOK, TOK), F32)
     scratch = [
@@ -516,8 +532,8 @@
         pltpu.VMEM((QW, 2 * TOK), BF),
         pltpu.VMEM((QW, 2 * TOK), BF),
         pltpu.VMEM((QW, 2 * TOK), BF),
-        pltpu.VMEM((rows, 2 * TOK), BF),
-        pltpu.VMEM((rows, 2 * TOK), BF),
+        pltpu.VMEM((D, 2 * TOK), BF),
+        pltpu.VMEM((D, 2 * TOK), BF),
         pltpu.VMEM((2, D, ALL), BF),
         pltpu.VMEM((TOK, KV), BF),
         pltpu.VMEM((TOK, KV), BF),
@@ -529,12 +545,12 @@
         pltpu.VMEM((2, ZN, plan.chunk, lanes), BF),
         pltpu.VMEM((2, plan.chunk, lanes), BF),
         pltpu.VMEM((3, 2, plan.chunk, lanes), BF),
-        pltpu.VMEM((2, plan.chunk, 2 * KV), F32),
         pltpu.VMEM((4, D // 4, TOK), BF),
-        pltpu.VMEM((4, D // 4, TOK), BF),
+        pltpu.VMEM((3, 2, D // 8, TOK), BF),
+        pltpu.VMEM((2, D // 8, TOK), BF),
         dma((16,)), dma((3,)), dma((3,)),
         dma((2, 2)), dma((2, 2)), dma((ZN, 2)), dma((ZN, 2)),
-        dma, dma, dma((ZN,)), dma((ZN,)), dma((2,)), dma((2,)), dma((4,)), dma((4,)),
+        dma, dma, dma((ZN,)), dma((ZN,)), dma((2,)), dma((2,)), dma((3, 2)), dma((3, 2)),
         dma((2, 2, 4)), dma((2, 2, 4)), dma((2, ZN)), dma((2, ZN)), dma((3, 2)), dma((3, 2)),
     ]
     gt, gw, go = pl.pallas_call(
@@ -555,9 +571,8 @@
     hold = pl.pallas_call(
         write_out,
         out_shape=tuple(jax.ShapeDtypeStruct(a.shape, a.dtype) for a in (gt, gw, go)),
-        in_specs=[hbm] * 3,
-        out_specs=(hbm, hbm, hbm),
-        scratch_shapes=[dma((3,))],
+        in_specs=[vm] * 3,
+        out_specs=(vm, vm, vm),
         compiler_params=pltpu.CompilerParams(vmem_limit_bytes=VMEM_BYTES),
     )(gt, gw, go)
     return hold[0].T, hold[1], hold[2].T

time: 53.3 us -> 46.3 us (0.87)
  Pallas kernels: 52.5 us -> 45.4 us
    pallas_call x1, Pallas kernels: 47.6 us -> 43.9 us  [per_device(): pl.pallas_call(functools.partial(body, plan), out_shape=(jax.ShapeDtypeSt...]
    pallas_call x1, Pallas kernels: 4.98 us -> 1.56 us  [per_device(): pl.pallas_call(write_out, out_shape=tuple((jax.ShapeDtypeStruct(a.shape,...]
where the time goes in v4:
time: 46.3 us; the launch traced here: 46.1 us
  Pallas kernels  45.4 us (98%)
  between operations  0.64 us (1%)
    pallas_call x1, Pallas kernels, per_device(): pl.pallas_call(functools.partial(body, plan), out_shape=(jax.ShapeDtypeSt...  43.9 us
    pallas_call x1, Pallas kernels, per_device(): pl.pallas_call(write_out, out_shape=tuple((jax.ShapeDtypeStruct(a.shape,...  1.56 us

profile of v4, /device:TPU:1, one launch (start us, length us, event | category | flops | bytes accessed | tf_op | source)
XLA Modules:
  0.0 46.1 jit_solution(10891751507791508657)
XLA Ops:
  0.6 43.9 %shard_map.85 = (bf16[192,256]{1,0:T(8,128)(2,1)}, f32[6,576]{1,0:T(8,128)}, f32[6,192]{1,0:T(8,128)}) custom-call(s32[2,4]{1,0:T(2,128)} %bitcast.8, s32[1,256]{1,0:T(1,128)} %bitcast.9, bf16[256,768]{1,0:T(8,128)(2,1)} %tokens_h.1, bf16[576,768]{1,0:T(8,128)(2,1)} %bitcast.5, bf16[192,768]{1,0:T(8,128)(2,1)} %wout_h.1, bf16[256,768]{1,0:T(8,128)(2,1)} %ograd_h.1), custom_call_target="tpu_custom_call" | custom-call | flops 2000000000 | bytes 4000000 | tf_op jit(solution)/shard_map/pallas_call | solution.py:556
  44.5 1.6 %shard_map.86 = (bf16[192,256]{1,0:T(8,128)(2,1)}, f32[6,576]{1,0:T(8,128)}, f32[6,192]{1,0:T(8,128)}) custom-call(bf16[192,256]{1,0:T(8,128)(2,1)} %get-tuple-element.9.gt, f32[6,576]{1,0:T(8,128)} %get-tuple-element.10.gw, f32[6,192]{1,0:T(8,128)} %get-tuple-element.11.go), custom_call_target="tpu_custom_call" | custom-call | tf_op jit(solution)/shard_map/pallas_call | solution.py:571

commit v5 on v4

--- a/solution.py
+++ b/solution.py
@@ -30,6 +30,7 @@
 ROWS3 = TOK // SPAN3
 PICKED = ROWS2 + ROWS3
 FAR_FIRST = (4, 3, 5, 2, 6, 1, 7)
+TURN = 2
 MARK = 2.0**100
 MARK_TEST = 2.0**90
 LOW = -1e30
@@ -84,11 +85,11 @@
 
 
 def body(plan, offs_h, valid_h, tokens_h, wqkv_h, wout_h, ograd_h, gt_out, gw_out, go_out,
-         offs, valid, tokens, wqkv, wout, ograd,
+         offs, valid, tokens, wqkv, wout, ograd, gt, gw, go,
          p_out, s2, s3, tok_in, og_in, proj, w_loc, p_loc, kv2, kv3, g2, g3, r2, r3, own, att_t, dq_t,
          dat_t, tok_t, og_t, wn, d_out, d_in, q_out, q_in,
          xs, xr, zs, zr, ys, yr, pt, pr, pv,
-         ls, es, er, a2s, a2r, a3s, a3r, b2s, b2r, b3s, b3r, ds_, dr_, cs, cr,
+         ls, os_, es, er, a2s, a2r, a3s, a3r, b2s, b2r, b3s, b3r, ds_, dr_, cs, cr,
          xss, xrs, zss, zrs, yss, yrs):
     xn, yn, nh = plan.xn, plan.yn, plan.n_head
     factor = 1.0 / math.sqrt(HD)
@@ -116,32 +117,36 @@
     if yn > 1:
         y_peers += [place(x, far, z, core), place(x, far, z, other)]
 
-    loads = []
-
-    def load(src, dst):
-        copy = pltpu.make_async_copy(src, dst, ls.at[len(loads)])
-        copy.start()
-        loads.append(copy)
-        return copy
-
-    def load_rows(src, dst, base, rows, pieces):
-        size = rows // pieces
-        return [load(src.at[at], dst.at[at]) for at in
-                [pl.ds(pl.multiple_of(base + size * i, 16), size) for i in range(pieces)]]
-
-    w_rows = MINE * 3 * HD
-    need_first = [load(valid_h, valid), load(offs_h, offs)]
-    need_first += load_rows(tokens_h, tokens, 0, TOK, 2)
-    need_first += load_rows(wqkv_h, wqkv, 0, CORES * w_rows, 4)
-    need_then = load_rows(ograd_h, ograd, 0, TOK, 2)
-    need_then += load_rows(wout_h, wout, 0, CORES * QW, 1)
-
     barrier = pltpu.get_barrier_semaphore()
     greeted = [place(x, y, zi, c) for zi in z_peers.values() for c in (core, other)] + y_peers
     greeted += [place(xi, y, z, core) for xi in x_peers.values()]
     greeted += [(seq, to) for to in h_peers.values()]
     for who in greeted:
         pl.semaphore_signal(barrier, inc=1, device_id=who, device_id_type=MESH)
+
+    loads = []
+
+    def load(src, dst):
+        copy = pltpu.make_async_copy(src, dst, ls.at[len(loads)])
+        copy.start()
+        loads.append(copy)
+        return copy
+
+    def load_rows(src, dst, base, rows, pieces):
+        size = rows // pieces
+        return [load(src.at[at], dst.at[at]) for at in
+                [pl.ds(pl.multiple_of(base + size * i, 16), size) for i in range(pieces)]]
+
+    w_rows = MINE * 3 * HD
+    need_first = load_rows(tokens_h, tokens, 0, TOK, 2)
+    for h in range(HEADS):
+        need_first += load_rows(wqkv_h, wqkv, 3 * HD * h + HD, 2 * HD, 1)
+    need_first += [load(valid_h, valid), load(offs_h, offs)]
+    need_then = []
+    for h in range(HEADS):
+        need_then += load_rows(wqkv_h, wqkv, 3 * HD * h, HD, 1)
+    need_then += load_rows(ograd_h, ograd, 0, TOK, 2)
+    need_then += load_rows(wout_h, wout, 0, CORES * QW, 1)
 
     started = []
 
@@ -153,28 +158,25 @@
         started.append(copy)
         return copy
 
-    def qkv_of(c):
-        base = c * w_rows
-        rows = [wqkv[pl.ds(pl.multiple_of(base + 3 * HD * h + HD, 16), 2 * HD), :]
-                for h in range(MINE)]
-        rows += [wqkv[pl.ds(pl.multiple_of(base + 3 * HD * h, 16), HD), :]
-                 for h in range(MINE)]
-        return jnp.concatenate(rows, axis=0)
+    def rows_of(c, start, size):
+        base = c * w_rows + start
+        return jnp.concatenate(
+            [wqkv[pl.ds(pl.multiple_of(base + 3 * HD * h, 16), size), :] for h in range(MINE)],
+            axis=0)
 
     def out_of(c):
         return wout[pl.ds(pl.multiple_of(c * QW, 16), QW), :]
 
     eye = iota((TOK, TOK), 0) == iota((TOK, TOK), 1)
     eye_b = one_hot(eye)
-    lane = iota((TOK, ALL), 1)
-    can_mark = (lane % (2 * HD) == 0) & (lane < KV)
+    can_mark = iota((TOK, KV), 1) % (2 * HD) == 0
     for copy in need_first:
         copy.wait()
     alive = jnp.sum(jnp.where(eye, valid[...].astype(F32), 0.0), axis=1, keepdims=True)
     marked = can_mark & (alive == 0.0)
-    w_mine, w_other = qkv_of(core), qkv_of(other)
-    proj[0, :, :ALL] = jnp.where(marked, MARK, nt(tokens[...], w_mine)).astype(BF)
-    p_out[:, :ALL] = jnp.where(marked, MARK, nt(tokens[...], w_other)).astype(BF)
+    kv_mine, kv_other = rows_of(core, HD, 2 * HD), rows_of(other, HD, 2 * HD)
+    p_out[:, :KV] = jnp.where(marked, MARK, nt(tokens[...], kv_other)).astype(BF)
+    proj[0, :, :KV] = jnp.where(marked, MARK, nt(tokens[...], kv_mine)).astype(BF)
 
     def pick_of(g):
         rows = iota((PICKED, TOK), 0)
@@ -210,6 +212,8 @@
 
     for copy in need_then:
         copy.wait()
+    q_mine, q_other = rows_of(core, 0, HD), rows_of(other, 0, HD)
+    p_out[:, KV:ALL] = nt(tokens[...], q_other).astype(BF)
     p_out[:, ALL:] = nt(ograd[...], out_of(other)).astype(BF)
     swap = send(p_out, proj.at[1], es.at[0], er.at[0], sibling)
     tok_swap = send(tokens, tok_in, es.at[1], er.at[1], sibling)
@@ -217,6 +221,7 @@
 
     phase2 = [offs[0, core * MINE + h] for h in range(MINE)]
     phase3 = [offs[1, core * MINE + h] for h in range(MINE)]
+    proj[0, :, KV:ALL] = nt(tokens[...], q_mine).astype(BF)
     proj[0, :, ALL:] = nt(ograd[...], out_of(core)).astype(BF)
     dat_t[:, :TOK] = nt(out_of(core), ograd[...]).astype(BF)
     swap.wait_recv()
@@ -258,19 +263,18 @@
         few.append([[jnp.concatenate([pair[0][at], pair[1][at]], axis=0) for pair in chosen]
                     for at in (slice(0, ROWS2), slice(ROWS2, PICKED))])
 
-    half = D // 2
-    eye_half = one_hot(iota((half, half), 0) == iota((half, half), 1))
+    row = iota((D, 1), 0)
+    inner = (row % plan.xrows + (z + TURN) * plan.rows_chip) % plan.xrows
+    order = one_hot(iota((D, D), 1) == row - row % plan.xrows + inner)
 
     def turn(to, block, b):
-        for part in range(2):
-            at = slice(part * half, (part + 1) * half)
-            to[at, b * TOK:(b + 1) * TOK] = nt(eye_half, block[:, at]).astype(BF)
+        to[:, b * TOK:(b + 1) * TOK] = nt(order, block[...]).astype(BF)
 
     turn(tok_t, tokens, 0)
     turn(og_t, ograd, 0)
     eye_d = one_hot(iota((D, D), 0) == iota((D, D), 1))
-    wn[0] = nt(eye_d, w_mine).astype(BF)
-    wn[1] = nt(eye_d, w_other).astype(BF)
+    wn[0] = nt(eye_d, jnp.concatenate([kv_mine, q_mine], axis=0)).astype(BF)
+    wn[1] = nt(eye_d, jnp.concatenate([kv_other, q_other], axis=0)).astype(BF)
 
     for copy in a_copies:
         copy.wait_recv()
@@ -278,20 +282,25 @@
     lane = iota((1, 2 * TOK), 1)
     rows_far = [kv2[...].reshape(TOK, KV), kv3[...].reshape(TOK, KV)]
     cols_far = [nt(eye_kv, r).astype(BF) for r in rows_far]
-    scale_loc, delta_loc, dq_far = [], [], []
+    units = [(h, level) for h in range(MINE) for level in range(2)]
+    members = [[lane % SPAN2 == phase2[h], lane % SPAN3 == phase3[h]] for h in range(MINE)]
+    col = [columns(h) for h in range(MINE)]
+    soft_far = {u: soft(rows_far[u[1]][:, col[u[0]][0]], few[u[0]][u[1]][0]) for u in units}
+    prod_far = {u: nt(rows_far[u[1]][:, col[u[0]][1]], few[u[0]][u[1]][1]) for u in units}
+    num_far = {u: nn(cols_far[u[1]][col[u[0]][1], :], soft_far[u][1].astype(BF)) for u in units}
+    full = {}
+    for u in units:
+        peak, _, den = soft_far[u]
+        full[u] = nn(jnp.concatenate([stack_rows(thirds(peak) + thirds(den))]
+                                     + halves(num_far[u]), axis=0), spots[u[0]][u[1]])
+    scale_loc, delta_loc, wanted = [], [], []
     for h in range(MINE):
-        kc, vc, _, _ = columns(h)
-        inside = [lane % SPAN2 == phase2[h], lane % SPAN3 == phase3[h]]
-        peaks, dens, nums, far_w = [local[h][0]], [local[h][1]], [local[h][2]], []
+        peaks, dens, nums = [local[h][0]], [local[h][1]], [local[h][2]]
         for level in range(2):
-            peak, w, den = soft(rows_far[level][:, kc], few[h][level][0])
-            num = nn(cols_far[level][vc, :], w.astype(BF))
-            got = nn(jnp.concatenate([stack_rows(thirds(peak) + thirds(den))] + halves(num), axis=0),
-                     spots[h][level])
-            peaks.append(jnp.where(inside[level], got[0:1] + got[1:2] + got[2:3], LOW))
+            got = full[h, level]
+            peaks.append(jnp.where(members[h][level], got[0:1] + got[1:2] + got[2:3], LOW))
             dens.append(got[3:4] + got[4:5] + got[5:6])
             nums.append(got[16:16 + HD] + got[16 + HD:16 + 2 * HD])
-            far_w.append(w)
         top = jnp.maximum(jnp.maximum(peaks[0], peaks[1]), peaks[2])
         scales = [jnp.exp(peak - top) for peak in peaks]
         inv = 1.0 / sum(scale * den for scale, den in zip(scales, dens))
@@ -301,27 +310,25 @@
         delta = jnp.sum(dat_t[hr, :].astype(F32) * att.astype(F32), axis=0, keepdims=True)
         scale_loc.append(scales[0] * inv)
         delta_loc.append(delta)
-        wanted = stack_rows(thirds(scales[1] * inv) + thirds(scales[2] * inv) + thirds(delta))
-        dq = None
-        for level, (to, n) in enumerate(((g2, PAIR), (g3, ZN))):
-            got = nt(wanted, spots[h][level])
-            i = 3 * level
-            scale = got[i:i + 1] + got[i + 1:i + 2] + got[i + 2:i + 3]
-            delta_few = got[6:7] + got[7:8] + got[8:9]
-            normed = far_w[level] * scale
-            q, d = few[h][level]
-            grad = (normed * (nt(rows_far[level][:, vc], d) - delta_few)).astype(BF)
-            dk = (nn(grad, q) * factor).astype(BF).reshape(n, CORES, -1, HD)
-            dv = nn(normed.astype(BF), d).astype(BF).reshape(n, CORES, -1, HD)
-            for part in range(CORES):
-                put = part * KV
-                to[:, :, put + kc.start:put + kc.stop] = dk[:, part]
-                to[:, :, put + vc.start:put + vc.stop] = dv[:, part]
-            back = nn(jnp.concatenate(halves(nn(cols_far[level][kc, :], grad)), axis=0),
-                      spots[h][level])
-            part = back[:HD] + back[HD:]
-            dq = part if dq is None else dq + part
-        dq_far.append(dq)
+        wanted.append(stack_rows(thirds(scales[1] * inv) + thirds(scales[2] * inv)
+                                 + thirds(delta)))
+    stats = {u: nt(wanted[u[0]], spots[u[0]][u[1]]) for u in units}
+    grads = {}
+    for u in units:
+        i, got = 3 * u[1], stats[u]
+        normed = soft_far[u][1] * (got[i:i + 1] + got[i + 1:i + 2] + got[i + 2:i + 3])
+        delta_few = got[6:7] + got[7:8] + got[8:9]
+        grads[u] = ((normed * (prod_far[u] - delta_few)).astype(BF), normed.astype(BF))
+    for u in units:
+        kc, vc, _, _ = col[u[0]]
+        q, d = few[u[0]][u[1]]
+        to, n = ((g2, PAIR), (g3, ZN))[u[1]]
+        dk = (nn(grads[u][0], q) * factor).astype(BF).reshape(n, CORES, -1, HD)
+        dv = nn(grads[u][1], d).astype(BF).reshape(n, CORES, -1, HD)
+        for part in range(CORES):
+            put = part * KV
+            to[:, :, put + kc.start:put + kc.stop] = dk[:, part]
+            to[:, :, put + vc.start:put + vc.stop] = dv[:, part]
 
     b_copies = []
     for d, zi in z_peers.items():
@@ -330,6 +337,14 @@
     r2[near_z] = g2[near_z]
     r3[z] = g3[z]
 
+    dq_far = []
+    for h in range(MINE):
+        parts = []
+        for level in range(2):
+            dq = nn(cols_far[level][col[h][0], :], grads[h, level][0])
+            dq = nn(jnp.concatenate(halves(dq), axis=0), spots[h][level])
+            parts.append(dq[:HD] + dq[HD:])
+        dq_far.append(parts[0] + parts[1])
     for h in range(MINE):
         kc, vc, qc, dc = columns(h)
         for b in range(2):
@@ -366,29 +381,23 @@
             for d, copy in zip(x_peers, some):
                 copy.wait_recv()
                 total = total + xr[i, d, at].astype(F32)
-            for j in range(deep):
+            here = [(k * deep + j + TURN) % ZN for j in range(deep)]
+            for j, d in enumerate(here):
                 rows = total[j * plan.rows_chip:(j + 1) * plan.rows_chip]
                 if plan.chunk > plan.rows_chip:
                     rest = jnp.zeros((plan.chunk - plan.rows_chip, plan.lanes), F32)
                     rows = jnp.concatenate([rows, rest], axis=0)
-                zs[i, k * deep + j] = rows.astype(BF)
+                zs[i, d] = rows.astype(BF)
             for d, zi in z_peers.items():
-                copy = pltpu.make_async_remote_copy(
-                    src_ref=zs.at[i, zi], dst_ref=zr.at[i, d], send_sem=zss.at[i, d],
-                    recv_sem=zrs.at[i, d], device_id=place(x, y, zi, core),
-                    device_id_type=MESH)
-                flying[d] = copy
-                if len(parts) == 1:
-                    copy.start()
-                else:
-                    pl.when(zi // deep == k)(copy.start)
-            if between is not None and k == 0:
-                between()
-        started.extend(flying.values())
+                if d in here:
+                    flying[d] = send(zs.at[i, d], zr.at[i, d], zss.at[i, d], zrs.at[i, d],
+                                     place(x, y, zi, core))
+        if between is not None:
+            between()
         return flying
 
     def start_y(i, copies):
-        total = zs[i, z].astype(F32)
+        total = zs[i, 0].astype(F32)
         for d, copy in copies.items():
             copy.wait_recv()
             total = total + zr[i, d].astype(F32)
@@ -470,7 +479,9 @@
         low = total[:cut] + pr[2, 0].astype(F32) + pr[1, 1].astype(F32)
         high = total[cut:] + pr[2, 1].astype(F32) + pr[1, 0].astype(F32)
         total = jnp.concatenate([low, high], axis=0)
-    gt_out[...] = total.astype(BF)
+    gt[...] = total.astype(BF)
+    stores = [pltpu.make_async_copy(gt, gt_out, os_.at[0])]
+    stores[0].start()
 
     sums = []
     for i, copies in enumerate((y_first, y_second)):
@@ -489,23 +500,37 @@
         sums.append([jnp.where(core == 0, own_part, far_part),
                      jnp.where(core == 0, far_part, own_part)])
     early, late = sums
-    go_out[...] = jnp.concatenate([early[c][:, :QW] for c in range(CORES)], axis=1)
-    gw_out[...] = jnp.concatenate(
+    go[...] = jnp.concatenate([early[c][:, :QW] for c in range(CORES)], axis=1)
+    gw[...] = jnp.concatenate(
         [piece for c in range(CORES) for h in range(MINE)
          for piece in (early[c][:, QW + HD * h:QW + HD * (h + 1)],
                        late[c][:, 2 * HD * h:2 * HD * (h + 1)])], axis=1)
+    stores.append(pltpu.make_async_copy(gw, gw_out, os_.at[1]))
+    stores.append(pltpu.make_async_copy(go, go_out, os_.at[2]))
+    for copy in stores[1:]:
+        copy.start()
     for copy in started:
         copy.wait_send()
-
-
-def write_out(gt, gw, go, gt_out, gw_out, go_out):
-    gt_out[...] = gt[...]
-    gw_out[...] = gw[...]
-    go_out[...] = go[...]
+    for copy in stores:
+        copy.wait()
+
+
+def write_out(*refs):
+    sources, results, stage, sems = refs[:3], refs[3:6], refs[6:9], refs[9]
+    loads = [pltpu.make_async_copy(a, b, sems.at[0, i])
+             for i, (a, b) in enumerate(zip(sources, stage))]
+    stores = [pltpu.make_async_copy(a, b, sems.at[1, i])
+              for i, (a, b) in enumerate(zip(stage, results))]
+    for copy in loads:
+        copy.start()
+    for load, store in zip(loads, stores):
+        load.wait()
+        store.start()
+    for copy in stores:
+        copy.wait()
 
 
 def per_device(plan, tokens, valid, offsets, qkv_weight, out_weight, out_grad):
-    vm = pl.BlockSpec(memory_space=pltpu.VMEM)
     hbm = pl.BlockSpec(memory_space=pltpu.HBM)
     dma = pltpu.SemaphoreType.DMA
     xn, lanes = plan.xn, plan.lanes
@@ -518,6 +543,9 @@
         pltpu.VMEM((HEADS * 3 * HD, D), BF),
         pltpu.VMEM((HEADS * HD, D), BF),
         pltpu.VMEM((TOK, D), BF),
+        pltpu.VMEM((D // 4, TOK), BF),
+        pltpu.VMEM((plan.rows_dev, HEADS * 3 * HD), F32),
+        pltpu.VMEM((plan.rows_dev, HEADS * HD), F32),
         pltpu.VMEM((TOK, ALL + QW), BF),
         pltpu.VMEM((ROWS2, KV), BF),
         pltpu.VMEM((ROWS3, KV), BF),
@@ -548,7 +576,7 @@
         pltpu.VMEM((4, D // 4, TOK), BF),
         pltpu.VMEM((3, 2, D // 8, TOK), BF),
         pltpu.VMEM((2, D // 8, TOK), BF),
-        dma((16,)), dma((3,)), dma((3,)),
+        dma((16,)), dma((3,)), dma((3,)), dma((3,)),
         dma((2, 2)), dma((2, 2)), dma((ZN, 2)), dma((ZN, 2)),
         dma, dma, dma((ZN,)), dma((ZN,)), dma((2,)), dma((2,)), dma((3, 2)), dma((3, 2)),
         dma((2, 2, 4)), dma((2, 2, 4)), dma((2, ZN)), dma((2, ZN)), dma((3, 2)), dma((3, 2)),
@@ -561,7 +589,7 @@
             jax.ShapeDtypeStruct((plan.rows_dev, HEADS * HD), F32),
         ),
         in_specs=[hbm] * 6,
-        out_specs=(vm, vm, vm),
+        out_specs=(hbm, hbm, hbm),
         scratch_shapes=scratch,
         compiler_params=pltpu.CompilerParams(
             collective_id=0, has_side_effects=True, vmem_limit_bytes=VMEM_BYTES),
@@ -571,8 +599,9 @@
     hold = pl.pallas_call(
         write_out,
         out_shape=tuple(jax.ShapeDtypeStruct(a.shape, a.dtype) for a in (gt, gw, go)),
-        in_specs=[vm] * 3,
-        out_specs=(vm, vm, vm),
+        in_specs=[hbm] * 3,
+        out_specs=(hbm, hbm, hbm),
+        scratch_shapes=[pltpu.VMEM(a.shape, a.dtype) for a in (gt, gw, go)] + [dma((2, 3))],
         compiler_params=pltpu.CompilerParams(vmem_limit_bytes=VMEM_BYTES),
     )(gt, gw, go)
     return hold[0].T, hold[1], hold[2].T

time: 46.3 us -> 44.3 us (0.957)
  Pallas kernels: 45.4 us -> 43.5 us
    pallas_call x1, Pallas kernels: 43.9 us -> 41.9 us  [per_device(): pl.pallas_call(functools.partial(body, plan), out_shape=(jax.ShapeDtypeSt...]
where the time goes in v5:
time: 44.3 us; the launch traced here: 44.1 us
  Pallas kernels  43.5 us (98%)
  between operations  0.64 us (1%)
    pallas_call x1, Pallas kernels, per_device(): pl.pallas_call(functools.partial(body, plan), out_shape=(jax.ShapeDtypeSt...  41.9 us
    pallas_call x1, Pallas kernels, per_device(): pl.pallas_call(write_out, out_shape=tuple((jax.ShapeDtypeStruct(a.shape,...  1.59 us

profile of v5, /device:TPU:1, one launch (start us, length us, event | category | flops | bytes accessed | tf_op | source)
XLA Modules:
  0.0 44.1 jit_solution(2201990175230214265)
XLA Ops:
  0.6 41.9 %shard_map.85 = (bf16[192,256]{1,0:T(8,128)(2,1)}, f32[6,576]{1,0:T(8,128)}, f32[6,192]{1,0:T(8,128)}) custom-call(s32[2,4]{1,0:T(2,128)} %bitcast.8, s32[1,256]{1,0:T(1,128)} %bitcast.9, bf16[256,768]{1,0:T(8,128)(2,1)} %tokens_h.1, bf16[576,768]{1,0:T(8,128)(2,1)} %bitcast.5, bf16[192,768]{1,0:T(8,128)(2,1)} %wout_h.1, bf16[256,768]{1,0:T(8,128)(2,1)} %ograd_h.1), custom_call_target="tpu_custom_call" | custom-call | flops 2000000000 | bytes 4000000 | tf_op jit(solution)/shard_map/pallas_call | solution.py:584
  42.6 1.6 %shard_map.86 = (bf16[192,256]{1,0:T(8,128)(2,1)}, f32[6,576]{1,0:T(8,128)}, f32[6,192]{1,0:T(8,128)}) custom-call(bf16[192,256]{1,0:T(8,128)(2,1)} %get-tuple-element.9.refs_0_, f32[6,576]{1,0:T(8,128)} %get-tuple-element.10.refs_1_, f32[6,192]{1,0:T(8,128)} %get-tuple-element.11.refs_2_), custom_call_target="tpu_custom_call" | custom-call | tf_op jit(solution)/shard_map/pallas_call | solution.py:599

commit v6 on v5

--- a/solution.py
+++ b/solution.py
@@ -72,6 +72,18 @@
     return [high, (x - high.astype(F32)).astype(BF)]
 
 
+def fold(rows):
+    n = rows.shape[0] // 2
+    return jnp.concatenate(
+        [rows[:, :128], jnp.concatenate([rows[:n, 128:], rows[n:, 128:]], axis=1)], axis=0)
+
+
+def unfold(rows):
+    n = 2 * rows.shape[0] // 3
+    return jnp.concatenate(
+        [rows[:n], jnp.concatenate([rows[n:, :64], rows[n:, 64:]], axis=0)], axis=1)
+
+
 class Plan:
     def __init__(self, n_seq, n_head):
         self.n_head = n_head
@@ -185,30 +197,39 @@
         return one_hot(iota((PICKED, TOK), 1) == want)
 
     picks = [pick_of(core * MINE + h) for h in range(MINE)]
-    for h in range(MINE):
-        cols = slice(2 * HD * h, 2 * HD * (h + 1))
-        chosen = nn(picks[h], proj[0, :, cols]).astype(BF)
-        kv2[pos2, :, cols] = chosen[:ROWS2]
-        kv3[pos3, :, cols] = chosen[ROWS2:]
-        chosen = nn(pick_of(other * MINE + h), p_out[:, cols]).astype(BF)
-        s2[:, cols] = chosen[:ROWS2]
-        s3[:, cols] = chosen[ROWS2:]
+    def choose(which, rows):
+        return jnp.concatenate(
+            [nn(which[h], rows[:, 2 * HD * h:2 * HD * (h + 1)]) for h in range(MINE)],
+            axis=1).astype(BF)
+
+    chosen = choose([pick_of(other * MINE + h) for h in range(MINE)], p_out[:, :KV])
+    s2[...] = fold(chosen[:ROWS2])
+    s3[...] = chosen[ROWS2:]
+    chosen = choose(picks, proj[0, :, :KV])
+    kv2[pos2] = fold(chosen[:ROWS2])
+    kv3[pos3] = chosen[ROWS2:]
 
     pl.semaphore_wait(barrier, len(greeted))
-    a_copies = []
-
-    def give(source, other_source, to, sems, at, slot, zi, c):
+    near_copies, wide_copies = [], []
+
+    def give_wide(d, zi, c):
         same = 0 if c is other else 1
-        a_copies.append(send(source if same else other_source, to.at[slot + 1 - same],
-                             sems[0].at[at, same], sems[1].at[at, same], place(x, y, zi, c)))
+        wide_copies.append(send(kv3.at[pos3] if same else s3, kv3.at[pos3 + 1 - same],
+                                a3s.at[d, same], a3r.at[d, same], place(x, y, zi, c)))
+
+    def give_near(at, zi, c):
+        same = 0 if c is other else 1
+        near_copies.append(send(kv2.at[pos2] if same else s2, kv2.at[pos2 + 1 - same],
+                                a2s.at[at, same], a2r.at[at, same], place(x, y, zi, c)))
 
     for d, zi in z_peers.items():
         for c in (core, other):
-            give(kv3.at[pos3], s3, kv3, (a3s, a3r), d, pos3, zi, c)
-    for c in (core, other):
-        give(kv2.at[pos2], s2, kv2, (a2s, a2r), 1, pos2, mate, c)
-    give(kv3.at[pos3], s3, kv3, (a3s, a3r), 0, pos3, z, other)
-    give(kv2.at[pos2], s2, kv2, (a2s, a2r), 0, pos2, z, other)
+            give_wide(d, zi, c)
+        if d == FAR_FIRST[2]:
+            for c in (core, other):
+                give_near(1, mate, c)
+    give_near(0, z, other)
+    give_wide(0, z, other)
 
     for copy in need_then:
         copy.wait()
@@ -276,23 +297,29 @@
     wn[0] = nt(eye_d, jnp.concatenate([kv_mine, q_mine], axis=0)).astype(BF)
     wn[1] = nt(eye_d, jnp.concatenate([kv_other, q_other], axis=0)).astype(BF)
 
-    for copy in a_copies:
-        copy.wait_recv()
-
     lane = iota((1, 2 * TOK), 1)
-    rows_far = [kv2[...].reshape(TOK, KV), kv3[...].reshape(TOK, KV)]
-    cols_far = [nt(eye_kv, r).astype(BF) for r in rows_far]
-    units = [(h, level) for h in range(MINE) for level in range(2)]
     members = [[lane % SPAN2 == phase2[h], lane % SPAN3 == phase3[h]] for h in range(MINE)]
     col = [columns(h) for h in range(MINE)]
-    soft_far = {u: soft(rows_far[u[1]][:, col[u[0]][0]], few[u[0]][u[1]][0]) for u in units}
-    prod_far = {u: nt(rows_far[u[1]][:, col[u[0]][1]], few[u[0]][u[1]][1]) for u in units}
-    num_far = {u: nn(cols_far[u[1]][col[u[0]][1], :], soft_far[u][1].astype(BF)) for u in units}
-    full = {}
-    for u in units:
-        peak, _, den = soft_far[u]
-        full[u] = nn(jnp.concatenate([stack_rows(thirds(peak) + thirds(den))]
-                                     + halves(num_far[u]), axis=0), spots[u[0]][u[1]])
+    units = [(h, level) for h in range(MINE) for level in range(2)]
+    rows_far, cols_far, soft_far, prod_far, full = [], [], {}, {}, {}
+    for level in range(2):
+        for copy in (near_copies, wide_copies)[level]:
+            copy.wait_recv()
+        if level == 0:
+            rows_far.append(jnp.concatenate([unfold(kv2[i]) for i in range(PAIR * CORES)], axis=0))
+        else:
+            rows_far.append(kv3[...].reshape(TOK, KV))
+        cols_far.append(nt(eye_kv, rows_far[level]).astype(BF))
+        for h in range(MINE):
+            kc, vc, _, _ = col[h]
+            q, d = few[h][level]
+            soft_far[h, level] = soft(rows_far[level][:, kc], q)
+            prod_far[h, level] = nt(rows_far[level][:, vc], d)
+        for h in range(MINE):
+            peak, w, den = soft_far[h, level]
+            num = nn(cols_far[level][col[h][1], :], w.astype(BF))
+            full[h, level] = nn(jnp.concatenate(
+                [stack_rows(thirds(peak) + thirds(den))] + halves(num), axis=0), spots[h][level])
     scale_loc, delta_loc, wanted = [], [], []
     for h in range(MINE):
         peaks, dens, nums = [local[h][0]], [local[h][1]], [local[h][2]]
@@ -392,8 +419,8 @@
                 if d in here:
                     flying[d] = send(zs.at[i, d], zr.at[i, d], zss.at[i, d], zrs.at[i, d],
                                      place(x, y, zi, core))
-        if between is not None:
-            between()
+            if between is not None:
+                between(k)
         return flying
 
     def start_y(i, copies):
@@ -438,8 +465,23 @@
     d_out[...] = theirs
     swap = send(d_out, d_in, ds_.at[1], dr_.at[1], sibling)
     mine = finish(0)
-    pack(1, 0, nn(tok_t[...], jnp.concatenate([mine, theirs], axis=0)))
-    x_second = start_x(1)
+    both = jnp.concatenate([mine, theirs], axis=0)
+    rows_x = yn * plan.xrows
+    x_late = [{}, {}]
+    for d in list(x_peers) + [0]:
+        xi = (x + d) % xn
+        block = nn(tok_t[pl.ds(pl.multiple_of(xi * rows_x, 16), rows_x), :], both).astype(BF)
+        for yi in range(yn):
+            xs[1, xi, :, yi * KV:(yi + 1) * KV] = block[yi * plan.xrows:(yi + 1) * plan.xrows]
+        if d:
+            k, at = parts_of(1)[0]
+            x_late[k][d] = send(xs.at[1, xi, at], xr.at[1, d, at], xss.at[1, k, d],
+                                xrs.at[1, k, d], place(xi, y, z, core))
+    for d, xi in x_peers.items():
+        k, at = parts_of(1)[1]
+        x_late[k][d] = send(xs.at[1, xi, at], xr.at[1, d, at], xss.at[1, k, d],
+                            xrs.at[1, k, d], place(xi, y, z, core))
+    x_second = [list(some.values()) for some in x_late]
 
     shares = nt(wn[0], jnp.concatenate([mine, dq[0]], axis=1))
     q_swap.wait_recv()
@@ -452,20 +494,28 @@
         ring = [((head + 1) % nh, 0), ((head + nh - 1) % nh, 1)]
         over = (head + 2) % nh
 
-        def hand(src, slot, way, to):
-            return send(src, pr.at[slot, way], cs.at[slot, way], cr.at[slot, way], (seq, to))
-
-        for to, way in ring:
-            c_far.append(hand(pt.at[over, pl.ds(way * cut, cut)], 0, way, to))
+        def hand(src, slot, way, to, at=None, part=0):
+            dst = pr.at[slot, way] if at is None else pr.at[slot, way, at]
+            return send(src, dst, cs.at[slot, way, part], cr.at[slot, way, part], (seq, to))
+
+        for part in range(2):
+            for to, way in ring:
+                at = pl.ds(part * cut // 2, cut // 2)
+                c_far.append(hand(pt.at[over, pl.ds(way * cut + part * cut // 2, cut // 2)],
+                                  0, way, to, at, part))
         for to, way in ring:
             c_near.append(hand(pt.at[to, pl.ds((1 - way) * cut, cut)], 1, way, to))
 
-    def pass_on():
-        for copy, (to, way) in zip(c_far, ring if nh > 1 else []):
+    def pass_on(part):
+        for copy, (to, way) in zip(c_far[2 * part:2 * part + 2], ring if nh > 1 else []):
+            at = slice(part * cut // 2, (part + 1) * cut // 2)
             copy.wait_recv()
-            both = pt[to, way * cut:(way + 1) * cut].astype(F32) + pr[0, way].astype(F32)
-            pv[way] = both.astype(BF)
-            c_near.append(hand(pv.at[way], 2, way, to))
+            base = way * cut
+            sum_of = (pt[to, base + at.start:base + at.stop].astype(F32)
+                      + pr[0, way, at].astype(F32))
+            pv[way, at] = sum_of.astype(BF)
+            c_near.append(hand(pv.at[way, pl.ds(at.start, cut // 2)], 2, way, to,
+                               pl.ds(at.start, cut // 2), part))
 
     z_first = start_z(0, x_first)
     z_second = start_z(1, x_second, pass_on)
@@ -547,13 +597,13 @@
         pltpu.VMEM((plan.rows_dev, HEADS * 3 * HD), F32),
         pltpu.VMEM((plan.rows_dev, HEADS * HD), F32),
         pltpu.VMEM((TOK, ALL + QW), BF),
-        pltpu.VMEM((ROWS2, KV), BF),
+        pltpu.VMEM((ROWS2 * KV // 128, 128), BF),
         pltpu.VMEM((ROWS3, KV), BF),
         pltpu.VMEM((TOK, D), BF),
         pltpu.VMEM((TOK, D), BF),
         pltpu.VMEM((2, TOK, ALL + QW), BF),
         square, square,
-        pltpu.VMEM((PAIR * CORES, ROWS2, KV), BF),
+        pltpu.VMEM((PAIR * CORES, ROWS2 * KV // 128, 128), BF),
         pltpu.VMEM((ZN * CORES, ROWS3, KV), BF),
         near, wide, near, wide,
         pltpu.VMEM((2, TOK, KV), F32),
@@ -578,7 +628,7 @@
         pltpu.VMEM((2, D // 8, TOK), BF),
         dma((16,)), dma((3,)), dma((3,)), dma((3,)),
         dma((2, 2)), dma((2, 2)), dma((ZN, 2)), dma((ZN, 2)),
-        dma, dma, dma((ZN,)), dma((ZN,)), dma((2,)), dma((2,)), dma((3, 2)), dma((3, 2)),
+        dma, dma, dma((ZN,)), dma((ZN,)), dma((2,)), dma((2,)), dma((3, 2, 2)), dma((3, 2, 2)),
         dma((2, 2, 4)), dma((2, 2, 4)), dma((2, ZN)), dma((2, ZN)), dma((3, 2)), dma((3, 2)),
     ]
     gt, gw, go = pl.pallas_call(

time: 44.3 us -> 45 us (1.016)
  Pallas kernels: 43.5 us -> 44.2 us
    pallas_call x1, Pallas kernels: 41.9 us -> 42.6 us  [per_device(): pl.pallas_call(functools.partial(body, plan), out_shape=(jax.ShapeDtypeSt...]
where the time goes in v6:
time: 45 us; the launch traced here: 44.8 us
  Pallas kernels  44.2 us (98%)
  between operations  0.64 us (1%)
    pallas_call x1, Pallas kernels, per_device(): pl.pallas_call(functools.partial(body, plan), out_shape=(jax.ShapeDtypeSt...  42.6 us
    pallas_call x1, Pallas kernels, per_device(): pl.pallas_call(write_out, out_shape=tuple((jax.ShapeDtypeStruct(a.shape,...  1.59 us

profile of v6, /device:TPU:1, one launch (start us, length us, event | category | flops | bytes accessed | tf_op | source)
XLA Modules:
  0.0 44.8 jit_solution(2272008027074228104)
XLA Ops:
  0.6 42.6 %shard_map.85 = (bf16[192,256]{1,0:T(8,128)(2,1)}, f32[6,576]{1,0:T(8,128)}, f32[6,192]{1,0:T(8,128)}) custom-call(s32[2,4]{1,0:T(2,128)} %bitcast.8, s32[1,256]{1,0:T(1,128)} %bitcast.9, bf16[256,768]{1,0:T(8,128)(2,1)} %tokens_h.1, bf16[576,768]{1,0:T(8,128)(2,1)} %bitcast.5, bf16[192,768]{1,0:T(8,128)(2,1)} %wout_h.1, bf16[256,768]{1,0:T(8,128)(2,1)} %ograd_h.1), custom_call_target="tpu_custom_call" | custom-call | flops 2000000000 | bytes 4000000 | tf_op jit(solution)/shard_map/pallas_call | solution.py:634
  43.3 1.6 %shard_map.86 = (bf16[192,256]{1,0:T(8,128)(2,1)}, f32[6,576]{1,0:T(8,128)}, f32[6,192]{1,0:T(8,128)}) custom-call(bf16[192,256]{1,0:T(8,128)(2,1)} %get-tuple-element.9.refs_0_, f32[6,576]{1,0:T(8,128)} %get-tuple-element.10.refs_1_, f32[6,192]{1,0:T(8,128)} %get-tuple-element.11.refs_2_), custom_call_target="tpu_custom_call" | custom-call | tf_op jit(solution)/shard_map/pallas_call | solution.py:649

commit v7 on v5

--- a/solution.py
+++ b/solution.py
@@ -34,7 +34,7 @@
 MARK = 2.0**100
 MARK_TEST = 2.0**90
 LOW = -1e30
-VMEM_BYTES = 58 * 1024 * 1024
+VMEM_BYTES = 53 * 1024 * 1024 + 700 * 1024
 
 
 def nn(a, b):
@@ -85,11 +85,11 @@
 
 
 def body(plan, offs_h, valid_h, tokens_h, wqkv_h, wout_h, ograd_h, gt_out, gw_out, go_out,
-         offs, valid, tokens, wqkv, wout, ograd, gt, gw, go,
+         offs, valid, tokens, wqkv, wout, ograd,
          p_out, s2, s3, tok_in, og_in, proj, w_loc, p_loc, kv2, kv3, g2, g3, r2, r3, own, att_t, dq_t,
          dat_t, tok_t, og_t, wn, d_out, d_in, q_out, q_in,
          xs, xr, zs, zr, ys, yr, pt, pr, pv,
-         ls, os_, es, er, a2s, a2r, a3s, a3r, b2s, b2r, b3s, b3r, ds_, dr_, cs, cr,
+         ls, es, er, a2s, a2r, a3s, a3r, b2s, b2r, b3s, b3r, ds_, dr_, cs, cr,
          xss, xrs, zss, zrs, yss, yrs):
     xn, yn, nh = plan.xn, plan.yn, plan.n_head
     factor = 1.0 / math.sqrt(HD)
@@ -471,6 +471,10 @@
     z_second = start_z(1, x_second, pass_on)
     y_first = start_y(0, z_first)
     y_second = start_y(1, z_second)
+    flying = y_second + c_near
+    for copy in started:
+        if not any(copy is other_copy for other_copy in flying):
+            copy.wait_send()
 
     total = pt[head].astype(F32)
     for copy in c_near:
@@ -479,9 +483,7 @@
         low = total[:cut] + pr[2, 0].astype(F32) + pr[1, 1].astype(F32)
         high = total[cut:] + pr[2, 1].astype(F32) + pr[1, 0].astype(F32)
         total = jnp.concatenate([low, high], axis=0)
-    gt[...] = total.astype(BF)
-    stores = [pltpu.make_async_copy(gt, gt_out, os_.at[0])]
-    stores[0].start()
+    gt_out[...] = total.astype(BF)
 
     sums = []
     for i, copies in enumerate((y_first, y_second)):
@@ -500,37 +502,26 @@
         sums.append([jnp.where(core == 0, own_part, far_part),
                      jnp.where(core == 0, far_part, own_part)])
     early, late = sums
-    go[...] = jnp.concatenate([early[c][:, :QW] for c in range(CORES)], axis=1)
-    gw[...] = jnp.concatenate(
+    go_out[...] = jnp.concatenate([early[c][:, :QW] for c in range(CORES)], axis=1)
+    gw_out[...] = jnp.concatenate(
         [piece for c in range(CORES) for h in range(MINE)
          for piece in (early[c][:, QW + HD * h:QW + HD * (h + 1)],
                        late[c][:, 2 * HD * h:2 * HD * (h + 1)])], axis=1)
-    stores.append(pltpu.make_async_copy(gw, gw_out, os_.at[1]))
-    stores.append(pltpu.make_async_copy(go, go_out, os_.at[2]))
-    for copy in stores[1:]:
+    for copy in flying:
+        copy.wait_send()
+
+
+def write_out(*refs):
+    copies = [pltpu.make_async_copy(a, b, refs[6].at[i])
+              for i, (a, b) in enumerate(zip(refs[:3], refs[3:6]))]
+    for copy in copies:
         copy.start()
-    for copy in started:
-        copy.wait_send()
-    for copy in stores:
+    for copy in copies:
         copy.wait()
 
 
-def write_out(*refs):
-    sources, results, stage, sems = refs[:3], refs[3:6], refs[6:9], refs[9]
-    loads = [pltpu.make_async_copy(a, b, sems.at[0, i])
-             for i, (a, b) in enumerate(zip(sources, stage))]
-    stores = [pltpu.make_async_copy(a, b, sems.at[1, i])
-              for i, (a, b) in enumerate(zip(stage, results))]
-    for copy in loads:
-        copy.start()
-    for load, store in zip(loads, stores):
-        load.wait()
-        store.start()
-    for copy in stores:
-        copy.wait()
-
-
 def per_device(plan, tokens, valid, offsets, qkv_weight, out_weight, out_grad):
+    vm = pl.BlockSpec(memory_space=pltpu.VMEM)
     hbm = pl.BlockSpec(memory_space=pltpu.HBM)
     dma = pltpu.SemaphoreType.DMA
     xn, lanes = plan.xn, plan.lanes
@@ -543,9 +534,6 @@
         pltpu.VMEM((HEADS * 3 * HD, D), BF),
         pltpu.VMEM((HEADS * HD, D), BF),
         pltpu.VMEM((TOK, D), BF),
-        pltpu.VMEM((D // 4, TOK), BF),
-        pltpu.VMEM((plan.rows_dev, HEADS * 3 * HD), F32),
-        pltpu.VMEM((plan.rows_dev, HEADS * HD), F32),
         pltpu.VMEM((TOK, ALL + QW), BF),
         pltpu.VMEM((ROWS2, KV), BF),
         pltpu.VMEM((ROWS3, KV), BF),
@@ -576,7 +564,7 @@
         pltpu.VMEM((4, D // 4, TOK), BF),
         pltpu.VMEM((3, 2, D // 8, TOK), BF),
         pltpu.VMEM((2, D // 8, TOK), BF),
-        dma((16,)), dma((3,)), dma((3,)), dma((3,)),
+        dma((16,)), dma((3,)), dma((3,)),
         dma((2, 2)), dma((2, 2)), dma((ZN, 2)), dma((ZN, 2)),
         dma, dma, dma((ZN,)), dma((ZN,)), dma((2,)), dma((2,)), dma((3, 2)), dma((3, 2)),
         dma((2, 2, 4)), dma((2, 2, 4)), dma((2, ZN)), dma((2, ZN)), dma((3, 2)), dma((3, 2)),
@@ -589,7 +577,7 @@
             jax.ShapeDtypeStruct((plan.rows_dev, HEADS * HD), F32),
         ),
         in_specs=[hbm] * 6,
-        out_specs=(hbm, hbm, hbm),
+        out_specs=(vm, vm, vm),
         scratch_shapes=scratch,
         compiler_params=pltpu.CompilerParams(
             collective_id=0, has_side_effects=True, vmem_limit_bytes=VMEM_BYTES),
@@ -599,10 +587,10 @@
     hold = pl.pallas_call(
         write_out,
         out_shape=tuple(jax.ShapeDtypeStruct(a.shape, a.dtype) for a in (gt, gw, go)),
-        in_specs=[hbm] * 3,
+        in_specs=[vm] * 3,
         out_specs=(hbm, hbm, hbm),
-        scratch_shapes=[pltpu.VMEM(a.shape, a.dtype) for a in (gt, gw, go)] + [dma((2, 3))],
-        compiler_params=pltpu.CompilerParams(vmem_limit_bytes=VMEM_BYTES),
+        scratch_shapes=[dma((3,))],
+        compiler_params=pltpu.CompilerParams(vmem_limit_bytes=1024 * 1024),
     )(gt, gw, go)
     return hold[0].T, hold[1], hold[2].T
 

time: 44.3 us -> 43.5 us (0.982)
  Pallas kernels: 43.5 us -> 42 us
  local copies, waits for them, and re-layouts: 0 us -> 0.68 us
    pallas_call x1, Pallas kernels: 1.59 us -> 0.67 us  [per_device(): pl.pallas_call(write_out, out_shape=tuple((jax.ShapeDtypeStruct(a.shape,...]
    unnamed x0 -> x4, local copies, waits for them, and re-layouts: none -> 0.68 us
    pallas_call x1, Pallas kernels: 41.9 us -> 41.3 us  [per_device(): pl.pallas_call(functools.partial(body, plan), out_shape=(jax.ShapeDtypeSt...]
where the time goes in v7:
time: 43.5 us; the launch traced here: 43.3 us
  Pallas kernels  42 us (97%)
  local copies, waits for them, and re-layouts  0.68 us (2%)
  between operations  0.66 us (2%)
    pallas_call x1, Pallas kernels, per_device(): pl.pallas_call(functools.partial(body, plan), out_shape=(jax.ShapeDtypeSt...  41.3 us

profile of v7, /device:TPU:1, one launch (start us, length us, event | category | flops | bytes accessed | tf_op | source)
XLA Modules:
  0.0 43.3 jit_solution(15197940230165479904)
XLA Ops:
  0.6 0.0 copy-start.1
  0.6 0.0 copy-start
  0.7 0.7 %copy-done.1 = s32[256]{0:T(256)S(1)} copy-done((s32[256]{0:T(256)S(1)}, s32[256]{0:T(256)}, u32[]{:S(2)}) %copy-start.1) | copy-done | bytes 1048
  1.3 0.0 copy-done
  1.3 41.3 %shard_map.85 = (bf16[192,256]{1,0:T(8,128)(2,1)S(1)}, f32[6,576]{1,0:T(8,128)S(1)}, f32[6,192]{1,0:T(8,128)S(1)}) custom-call(s32[2,4]{1,0:T(2,128)S(1)} %bitcast.5, s32[1,256]{1,0:T(1,128)S(1)} %bitcast.6, bf16[256,768]{1,0:T(8,128)(2,1)} %tokens_h.1, bf16[576,768]{1,0:T(8,128)(2,1)} %bitcast.7, bf16[192,768]{1,0:T(8,128)(2,1)} %wout_h.1, ...), custom_call_target="tpu_custom_call" | custom-call | flops 2000000000 | bytes 4000000 | tf_op jit(solution)/shard_map/pallas_call | solution.py:572
  42.6 0.7 %shard_map.86 = (bf16[192,256]{1,0:T(8,128)(2,1)}, f32[6,576]{1,0:T(8,128)}, f32[6,192]{1,0:T(8,128)}) custom-call(bf16[192,256]{1,0:T(8,128)(2,1)S(1)} %get-tuple-element.9.refs_0_, f32[6,576]{1,0:T(8,128)S(1)} %get-tuple-element.10.refs_1_, f32[6,192]{1,0:T(8,128)S(1)} %get-tuple-element.11.refs_2_), custom_call_target="tpu_custom_call" | custom-call | tf_op jit(solution)/shard_map/pallas_call | solution.py:587
Async XLA Ops:
  0.6 0.7 %copy-start.1 = (s32[256]{0:T(256)S(1)}, s32[256]{0:T(256)}, u32[]{:S(2)}) copy-start(s32[256]{0:T(256)} %param.7) | copy-start | bytes 3076
  0.6 0.7 %copy-start = (s32[4,2]{0,1:T(2,128)S(1)}, s32[4,2]{0,1:T(2,128)}, u32[]{:S(2)}) copy-start(s32[4,2]{0,1:T(2,128)} %param.8) | copy-start | bytes 100

commit v8 on v7

--- a/solution.py
+++ b/solution.py
@@ -88,7 +88,7 @@
          offs, valid, tokens, wqkv, wout, ograd,
          p_out, s2, s3, tok_in, og_in, proj, w_loc, p_loc, kv2, kv3, g2, g3, r2, r3, own, att_t, dq_t,
          dat_t, tok_t, og_t, wn, d_out, d_in, q_out, q_in,
-         xs, xr, zs, zr, ys, yr, pt, pr, pv,
+         xs, xr, zs, zr, ys, yr, pt, pr, pv, ours,
          ls, es, er, a2s, a2r, a3s, a3r, b2s, b2r, b3s, b3r, ds_, dr_, cs, cr,
          xss, xrs, zss, zrs, yss, yrs):
     xn, yn, nh = plan.xn, plan.yn, plan.n_head
@@ -121,8 +121,12 @@
     greeted = [place(x, y, zi, c) for zi in z_peers.values() for c in (core, other)] + y_peers
     greeted += [place(xi, y, z, core) for xi in x_peers.values()]
     greeted += [(seq, to) for to in h_peers.values()]
-    for who in greeted:
-        pl.semaphore_signal(barrier, inc=1, device_id=who, device_id_type=MESH)
+    def greet(some):
+        for who in some:
+            pl.semaphore_signal(barrier, inc=1, device_id=who, device_id_type=MESH)
+
+    soon = CORES * len(z_peers) + 1
+    greet(greeted[:soon])
 
     loads = []
 
@@ -147,6 +151,8 @@
         need_then += load_rows(wqkv_h, wqkv, 3 * HD * h, HD, 1)
     need_then += load_rows(ograd_h, ograd, 0, TOK, 2)
     need_then += load_rows(wout_h, wout, 0, CORES * QW, 1)
+
+    greet(greeted[soon:])
 
     started = []
 
@@ -314,26 +320,32 @@
                                  + thirds(delta)))
     stats = {u: nt(wanted[u[0]], spots[u[0]][u[1]]) for u in units}
     grads = {}
-    for u in units:
-        i, got = 3 * u[1], stats[u]
-        normed = soft_far[u][1] * (got[i:i + 1] + got[i + 1:i + 2] + got[i + 2:i + 3])
-        delta_few = got[6:7] + got[7:8] + got[8:9]
-        grads[u] = ((normed * (prod_far[u] - delta_few)).astype(BF), normed.astype(BF))
-    for u in units:
-        kc, vc, _, _ = col[u[0]]
-        q, d = few[u[0]][u[1]]
-        to, n = ((g2, PAIR), (g3, ZN))[u[1]]
-        dk = (nn(grads[u][0], q) * factor).astype(BF).reshape(n, CORES, -1, HD)
-        dv = nn(grads[u][1], d).astype(BF).reshape(n, CORES, -1, HD)
-        for part in range(CORES):
-            put = part * KV
-            to[:, :, put + kc.start:put + kc.stop] = dk[:, part]
-            to[:, :, put + vc.start:put + vc.stop] = dv[:, part]
-
     b_copies = []
-    for d, zi in z_peers.items():
-        b_copies.append(send(g3.at[zi], r3.at[z], b3s.at[d], b3r.at[d], place(x, y, zi, core)))
-    b_copies.append(send(g2.at[1 - near_z], r2.at[near_z], b2s, b2r, place(x, y, mate, core)))
+    for level in (1, 0):
+        for h in range(MINE):
+            i, got = 3 * level, stats[h, level]
+            normed = soft_far[h, level][1] * (got[i:i + 1] + got[i + 1:i + 2] + got[i + 2:i + 3])
+            delta_few = got[6:7] + got[7:8] + got[8:9]
+            grads[h, level] = ((normed * (prod_far[h, level] - delta_few)).astype(BF),
+                               normed.astype(BF))
+        for h in range(MINE):
+            kc, vc, _, _ = col[h]
+            q, d = few[h][level]
+            to, n = ((g2, PAIR), (g3, ZN))[level]
+            dk = (nn(grads[h, level][0], q) * factor).astype(BF).reshape(n, CORES, -1, HD)
+            dv = nn(grads[h, level][1], d).astype(BF).reshape(n, CORES, -1, HD)
+            for part in range(CORES):
+                put = part * KV
+                to[:, :, put + kc.start:put + kc.stop] = dk[:, part]
+                to[:, :, put + vc.start:put + vc.stop] = dv[:, part]
+        if level:
+            for d, zi in z_peers.items():
+                b_copies.append(send(g3.at[zi], r3.at[z], b3s.at[d], b3r.at[d],
+                                     place(x, y, zi, core)))
+        else:
+            b_copies.append(send(g2.at[1 - near_z], r2.at[near_z], b2s, b2r,
+                                 place(x, y, mate, core)))
+
     r2[near_z] = g2[near_z]
     r3[z] = g3[z]
 
@@ -441,11 +453,15 @@
     pack(1, 0, nn(tok_t[...], jnp.concatenate([mine, theirs], axis=0)))
     x_second = start_x(1)
 
-    shares = nt(wn[0], jnp.concatenate([mine, dq[0]], axis=1))
+    ours[...] = nt(wn[0], jnp.concatenate([mine, dq[0]], axis=1)).reshape(ours.shape)
     q_swap.wait_recv()
     swap.wait_recv()
-    shares = shares + nt(wn[1], jnp.concatenate([d_in[...], q_in[...]], axis=1))
-    pt[...] = shares.astype(BF).reshape(pt.shape)
+    got_rows = jnp.concatenate([d_in[...], q_in[...]], axis=1)
+
+    def share(to):
+        rows = pl.ds(pl.multiple_of(to * (D // 4), 16), D // 4)
+        pt[to] = (ours[to] + nt(wn[1, rows, :], got_rows)).astype(BF)
+
     c_far, c_near = [], []
     cut = D // 8
     if nh > 1:
@@ -455,10 +471,13 @@
         def hand(src, slot, way, to):
             return send(src, pr.at[slot, way], cs.at[slot, way], cr.at[slot, way], (seq, to))
 
+        share(over)
         for to, way in ring:
             c_far.append(hand(pt.at[over, pl.ds(way * cut, cut)], 0, way, to))
         for to, way in ring:
+            share(to)
             c_near.append(hand(pt.at[to, pl.ds((1 - way) * cut, cut)], 1, way, to))
+    share(head)
 
     def pass_on():
         for copy, (to, way) in zip(c_far, ring if nh > 1 else []):
@@ -564,6 +583,7 @@
         pltpu.VMEM((4, D // 4, TOK), BF),
         pltpu.VMEM((3, 2, D // 8, TOK), BF),
         pltpu.VMEM((2, D // 8, TOK), BF),
+        pltpu.VMEM((4, D // 4, TOK), F32),
         dma((16,)), dma((3,)), dma((3,)),
         dma((2, 2)), dma((2, 2)), dma((ZN, 2)), dma((ZN, 2)),
         dma, dma, dma((ZN,)), dma((ZN,)), dma((2,)), dma((2,)), dma((3, 2)), dma((3, 2)),

time: 43.5 us -> 43.2 us (level)
  no operation moved by 1% of the time
where the time goes in v8:
time: 43.2 us; the launch traced here: 43.1 us
  Pallas kernels  41.7 us (97%)
  local copies, waits for them, and re-layouts  0.68 us (2%)
  between operations  0.66 us (2%)
    pallas_call x1, Pallas kernels, per_device(): pl.pallas_call(functools.partial(body, plan), out_shape=(jax.ShapeDtypeSt...  41.1 us

profile of v8, /device:TPU:1, one launch (start us, length us, event | category | flops | bytes accessed | tf_op | source)
XLA Modules:
  0.0 43.1 jit_solution(2292330620875457877)
XLA Ops:
  0.6 0.0 copy-start.1
  0.6 0.0 copy-start
  0.7 0.7 %copy-done.1 = s32[256]{0:T(256)S(1)} copy-done((s32[256]{0:T(256)S(1)}, s32[256]{0:T(256)}, u32[]{:S(2)}) %copy-start.1) | copy-done | bytes 1048
  1.3 0.0 copy-done
  1.3 41.1 %shard_map.85 = (bf16[192,256]{1,0:T(8,128)(2,1)S(1)}, f32[6,576]{1,0:T(8,128)S(1)}, f32[6,192]{1,0:T(8,128)S(1)}) custom-call(s32[2,4]{1,0:T(2,128)S(1)} %bitcast.5, s32[1,256]{1,0:T(1,128)S(1)} %bitcast.6, bf16[256,768]{1,0:T(8,128)(2,1)} %tokens_h.1, bf16[576,768]{1,0:T(8,128)(2,1)} %bitcast.7, bf16[192,768]{1,0:T(8,128)(2,1)} %wout_h.1, ...), custom_call_target="tpu_custom_call" | custom-call | flops 2000000000 | bytes 4000000 | tf_op jit(solution)/shard_map/pallas_call | solution.py:592
  42.4 0.7 %shard_map.86 = (bf16[192,256]{1,0:T(8,128)(2,1)}, f32[6,576]{1,0:T(8,128)}, f32[6,192]{1,0:T(8,128)}) custom-call(bf16[192,256]{1,0:T(8,128)(2,1)S(1)} %get-tuple-element.9.refs_0_, f32[6,576]{1,0:T(8,128)S(1)} %get-tuple-element.10.refs_1_, f32[6,192]{1,0:T(8,128)S(1)} %get-tuple-element.11.refs_2_), custom_call_target="tpu_custom_call" | custom-call | tf_op jit(solution)/shard_map/pallas_call | solution.py:607
Async XLA Ops:
  0.6 0.7 %copy-start.1 = (s32[256]{0:T(256)S(1)}, s32[256]{0:T(256)}, u32[]{:S(2)}) copy-start(s32[256]{0:T(256)} %param.7) | copy-start | bytes 3076
  0.6 0.7 %copy-start = (s32[4,2]{0,1:T(2,128)S(1)}, s32[4,2]{0,1:T(2,128)}, u32[]{:S(2)}) copy-start(s32[4,2]{0,1:T(2,128)} %param.8) | copy-start | bytes 100
